TPU v7x, 32 devices: a whole 2x2x4 slice. The times are simulated.
32 devices in a mesh: dp: 8 (over z, x), mp: 4 (over y, core).
Axes of the slice: x: 2, y: 2, z: 4, core: 2. Of those that a mesh axis runs over, the one named last changes fastest.
Arguments:
- features: bfloat16 [1024, 1536], P('dp', 'mp'), may hold values from -240 to 240
- proj_weight: bfloat16 [1536, 1152], P('mp'), may hold values from -0.15625 to 0.15625
- texts: bfloat16 [1024, 1152], P(('dp', 'mp')), may hold values from -6 to 6
Outputs:
- grad_features: bfloat16 [1024, 1536], P('dp', 'mp')
- grad_weight: float32 [1536, 1152], P('mp')
All inputs are finite; a program needn't handle non-finite values.
Results may differ from a plain program's by a relative error of at most 0.011.
Values may be sent and summed in bfloat16 or wider, within the bound.
No kernel may reach another device: no remote copies, remote signals or barrier semaphores. Data moves between devices by JAX's collectives and lax.ppermute only.
A program may use at most 64 MiB of HBM per device.

v0:
```python
import functools

import jax
import jax.numpy as jnp
from jax import lax
from jax.experimental import pallas as pl
from jax.experimental.pallas import tpu as pltpu
from jax.sharding import PartitionSpec as P

logit_scale = 100.0
logit_bias = -10.0
epsilon = 1e-06
LANES = 128
GATHER_BYTES = 8 << 20
VMEM_BYTES = 40 << 20


def unit_rows(values):
    return values * lax.rsqrt(jnp.sum(values * values, axis=1, keepdims=True) + epsilon)


def add_texts(unit_img_b, image_ids, piece, piece_ids):
    unit_txt_b = unit_rows(piece.astype(jnp.float32)).astype(jnp.bfloat16)
    logits = (
        logit_scale * jnp.dot(unit_img_b, unit_txt_b.T, preferred_element_type=jnp.float32)
        + logit_bias
    )
    labels = jnp.where(image_ids[:, None] == piece_ids[None, :], 1.0, -1.0).astype(jnp.float32)
    slopes = (-labels * jax.nn.sigmoid(-labels * logits)).astype(jnp.bfloat16)
    return logit_scale * jnp.dot(slopes, unit_txt_b, preferred_element_type=jnp.float32)


def shards_summed(features, proj_weight, texts):
    local_rows = features.shape[0]
    width_local = features.shape[1]
    mp_count = lax.axis_size("mp")
    full_width = width_local * mp_count
    mp_index = lax.axis_index("mp")
    dp_index = lax.axis_index("dp")
    text_rows = texts.shape[0]
    inputs = features.astype(jnp.float32)
    mean_in = lax.psum(jnp.sum(inputs, axis=1, keepdims=True), "mp") / full_width
    centred = inputs - mean_in
    normed_b = centred.astype(jnp.bfloat16)
    partial_proj = jnp.dot(normed_b, proj_weight, preferred_element_type=jnp.float32)
    project = lax.psum(partial_proj, "mp")
    inv_norm = lax.rsqrt(jnp.sum(project * project, axis=1, keepdims=True) + epsilon)
    unit_img = project * inv_norm
    unit_img_b = unit_img.astype(jnp.bfloat16)
    image_ids = dp_index * local_rows + jnp.arange(local_rows, dtype=jnp.int32)
    piece = lax.all_gather(texts, "dp", axis=0, tiled=True)
    positions = jnp.arange(piece.shape[0], dtype=jnp.int32)
    shard_of = positions // text_rows
    piece_ids = (shard_of * mp_count + mp_index) * text_rows + positions % text_rows
    grad_unit = add_texts(unit_img_b, image_ids, piece, piece_ids)
    grad_unit = lax.psum(grad_unit, "mp")
    grad_proj = inv_norm * (
        grad_unit - unit_img * jnp.sum(unit_img * grad_unit, axis=1, keepdims=True)
    )
    grad_proj_b = grad_proj.astype(jnp.bfloat16)
    weight_part = jnp.dot(normed_b.T, grad_proj_b, preferred_element_type=jnp.float32)
    grad_weight = lax.psum(weight_part, "dp")
    grad_normed = jnp.dot(grad_proj_b, proj_weight.T, preferred_element_type=jnp.float32)
    grad_total = lax.psum(jnp.sum(grad_normed, axis=1, keepdims=True), "mp")
    grad_in = grad_normed - grad_total / full_width
    return (grad_in.astype(jnp.bfloat16), grad_weight)


def split_terms(value, count):
    terms = []
    for _ in range(count):
        term = value.astype(jnp.bfloat16).astype(jnp.float32)
        terms.append(term)
        value = value - term
    return terms


def kernel_call(body, outs, scratch=(), flops=0, **names):
    return pl.pallas_call(
        body,
        out_shape=outs,
        scratch_shapes=scratch,
        compiler_params=pltpu.CompilerParams(vmem_limit_bytes=VMEM_BYTES),
        cost_estimate=pl.CostEstimate(flops=flops, bytes_accessed=0, transcendentals=0),
        **names,
    )


def texts_body(texts_ref, out_ref):
    out_ref[...] = unit_rows(texts_ref[...].astype(jnp.float32)).astype(jnp.bfloat16)


def store_sums(extra_ref, column_sum, sum_row):
    extra_ref[...] = jnp.zeros_like(extra_ref)
    at = 0
    for term in split_terms(column_sum, 2):
        for i in range(column_sum.shape[1] // LANES):
            extra_ref[at : at + 1, :] = term[:, i * LANES : (i + 1) * LANES]
            at += 1
    for term in split_terms(sum_row, 3):
        extra_ref[at : at + 1, :] = term
        at += 1
    return extra_ref[...].astype(jnp.bfloat16)


def load_sums(extra, embed):
    chunks = embed // LANES
    extra = extra.astype(jnp.float32)
    column_sum = jnp.concatenate(
        [extra[i : i + 1] + extra[chunks + i : chunks + i + 1] for i in range(chunks)], axis=1
    )
    at = 2 * chunks
    return column_sum, extra[at : at + 1] + extra[at + 1 : at + 2] + extra[at + 2 : at + 3]


def pick_rows(sum_row, rows, group):
    row = lax.broadcasted_iota(jnp.int32, (rows, LANES), 0)
    lane = lax.broadcasted_iota(jnp.int32, (rows, LANES), 1)
    return jnp.sum(jnp.where(lane == row + group * rows, sum_row, 0.0), axis=1, keepdims=True)


def project_body(
    rows, mp_count, place_ref, features_ref, weight_ref,
    keep_ref, send_ref, column_sum_ref, sum_row_ref, extra_ref,
):
    embed = weight_ref.shape[1]
    local_rows, width = features_ref.shape
    values = features_ref[...].astype(jnp.float32)
    row_sum = jnp.sum(values, axis=1, keepdims=True)
    column_sum = jnp.sum(weight_ref[...].astype(jnp.float32), axis=0, keepdims=True)
    row = lax.broadcasted_iota(jnp.int32, (local_rows, LANES), 0)
    lane = lax.broadcasted_iota(jnp.int32, (local_rows, LANES), 1)
    sum_row = jnp.sum(jnp.where(row == lane, row_sum, 0.0), axis=0, keepdims=True)
    ordered = []
    for flip in list(range(0, mp_count, 2)) + list(range(1, mp_count, 2)):
        start = pl.multiple_of(((place_ref[0] ^ flip) & (mp_count - 1)) * rows, rows)
        block = features_ref[pl.ds(start, rows), :].astype(jnp.float32)
        ordered.append(block - jnp.sum(block, axis=1, keepdims=True) / width)
    centred = jnp.concatenate(ordered, axis=0).astype(jnp.bfloat16)
    product = jnp.dot(centred, weight_ref[...], preferred_element_type=jnp.float32)
    half = local_rows // 2
    keep_ref[...] = product[:half]
    send_ref[:, :embed] = product[half:].astype(jnp.bfloat16)
    extra = store_sums(extra_ref, column_sum, sum_row)
    for i in range(half // rows):
        send_ref[i * rows : (i + 1) * rows, embed:] = extra
    column_sum_ref[...] = column_sum
    sum_row_ref[...] = sum_row


def chip_body(
    width, mp_count, place_ref, keep_ref, received_ref, column_sum_ref, sum_row_ref,
    own_ref, send_ref, chip_column_ref, chip_row_ref, extra_ref,
):
    rows = own_ref.shape[0]
    embed = own_ref.shape[1]
    columns = [column_sum_ref[...], None]
    sum_rows = [sum_row_ref[...], None]
    columns[1], sum_rows[1] = load_sums(received_ref[:rows, embed:], embed)
    chip_column = columns[0] + columns[1]
    chip_row = sum_rows[0] + sum_rows[1]
    for i in range(2):
        group = (place_ref[0] ^ (2 * i)) & (mp_count - 1)
        mean = pick_rows(chip_row, rows, group) / (2 * width)
        here = slice(i * rows, (i + 1) * rows)
        total = keep_ref[here, :] + received_ref[here, :embed].astype(jnp.float32)
        for column, sum_row in zip(columns, sum_rows):
            total = total + (pick_rows(sum_row, rows, group) / width - mean) * column
        if i == 0:
            own_ref[...] = total
        else:
            send_ref[:, :embed] = total.astype(jnp.bfloat16)
    send_ref[:, embed:] = store_sums(extra_ref, chip_column, chip_row)
    chip_column_ref[...] = chip_column
    chip_row_ref[...] = chip_row


def rows_body(
    full_width, mp_count, place_ref, own_ref, received_ref, column_sum_ref, sum_row_ref,
    project_ref, mean_ref, weight_sum_ref,
):
    rows, embed = own_ref.shape
    columns = [column_sum_ref[...], None]
    sum_rows = [sum_row_ref[...], None]
    columns[1], sum_rows[1] = load_sums(received_ref[:, embed:], embed)
    group = place_ref[0] & (mp_count - 1)
    full_row = sum_rows[0] + sum_rows[1]
    mean = pick_rows(full_row, rows, group) / full_width
    project = own_ref[...] + received_ref[:, :embed].astype(jnp.float32)
    for column, sum_row in zip(columns, sum_rows):
        part_mean = pick_rows(sum_row, rows, group) / (full_width // 2)
        project = project + (part_mean - mean) * column
    project_ref[...] = project.astype(jnp.bfloat16)
    mean_ref[...] = pick_rows(full_row, mean_ref.shape[0], 0) / full_width
    weight_sum_ref[...] = columns[0] + columns[1]


def centre_body(features_ref, mean_ref, out_ref):
    centred = features_ref[...].astype(jnp.float32) - mean_ref[...]
    out_ref[...] = centred.astype(jnp.bfloat16)


def grad_body(first, project_ref, *refs):
    (*texts, out_ref) = refs
    project = project_ref[...].astype(jnp.float32)
    inv_norm = lax.rsqrt(jnp.sum(project * project, axis=1, keepdims=True) + epsilon)
    unit_img = project * inv_norm
    unit_img_b = unit_img.astype(jnp.bfloat16)
    grad_unit = jnp.zeros_like(project)
    at = 0
    for ref in texts:
        unit_txt_b = ref[...]
        logits = (
            logit_scale
            * lax.dot_general(
                unit_img_b,
                unit_txt_b,
                (((1,), (1,)), ((), ())),
                preferred_element_type=jnp.float32,
            )
            + logit_bias
        )
        text = lax.broadcasted_iota(jnp.int32, logits.shape, 1) + at
        image = lax.broadcasted_iota(jnp.int32, logits.shape, 0) + first
        labels = jnp.where(text == image, 1.0, -1.0)
        slopes = (-labels / (1.0 + jnp.exp(labels * logits))).astype(jnp.bfloat16)
        grad_unit = grad_unit + jnp.dot(slopes, unit_txt_b, preferred_element_type=jnp.float32)
        at += unit_txt_b.shape[0]
    grad_unit = logit_scale * grad_unit
    grad_proj = inv_norm * (
        grad_unit - unit_img * jnp.sum(unit_img * grad_unit, axis=1, keepdims=True)
    )
    out_ref[...] = grad_proj.astype(jnp.bfloat16)


def weight_body(
    rows, mp_count, normed_order, orders, tiles, place_ref, normed_ref, *refs
):
    count = 2 * len(orders)
    arrays = refs[:count]
    previous = refs[count : count + 1] if len(refs) - count > (1 if tiles == 1 else 3) else ()
    outs = refs[count + len(previous) :]
    blocks = []
    for order in orders:
        for i in range(2):
            for flip in order:
                group = (place_ref[0] ^ flip ^ i) & (mp_count - 1)
                at = normed_order.index(flip - flip % mp_count) * mp_count
                start = pl.multiple_of((at + group) * rows, rows)
                blocks.append(normed_ref[pl.ds(start, rows), :])
    normed = jnp.concatenate(blocks, axis=0)
    gradient = jnp.concatenate([array[...] for array in arrays], axis=0)
    if tiles == 1:
        total = lax.dot_general(
            normed, gradient, (((0,), (0,)), ((), ())), preferred_element_type=jnp.float32
        )
        for ref in previous:
            total = total + ref[...]
        outs[0][...] = total
        return
    out_hbm, total_ref, sent = outs
    wide = gradient.shape[1] // tiles
    copies = []
    for k in range(tiles):
        here = slice(k * wide, (k + 1) * wide)
        total = lax.dot_general(
            normed, gradient[:, here], (((0,), (0,)), ((), ())), preferred_element_type=jnp.float32
        )
        for ref in previous:
            total = total + ref[:, here]
        total_ref[:, here] = total
        copies.append(
            pltpu.make_async_copy(total_ref.at[:, here], out_hbm.at[:, here], sent.at[k])
        )
        copies[-1].start()
    for copy in copies:
        copy.wait()


def features_body(full_width, rows, mp_count, place_ref, weight_ref, weight_sum_ref, *refs):
    (*parts, out_ref, group_ref) = refs
    for flip, part in enumerate(parts):
        start = pl.multiple_of(((place_ref[0] ^ flip) & (mp_count - 1)) * rows, rows)
        group_ref[pl.ds(start, rows), :] = part[:rows, :]
    group = group_ref[...]
    grad_normed = lax.dot_general(
        group, weight_ref[...], (((1,), (1,)), ((), ())), preferred_element_type=jnp.float32
    )
    grad_total = jnp.sum(group.astype(jnp.float32) * weight_sum_ref[...], axis=1, keepdims=True)
    out_ref[...] = (grad_normed - grad_total / full_width).astype(jnp.bfloat16)


def shards_gathered(features, proj_weight, texts):
    axes = ("dp", "mp")
    dp_count, mp_count = lax.axis_size("dp"), lax.axis_size("mp")
    count = dp_count * mp_count
    plane_count = 2 * mp_count
    local_rows, width = features.shape
    embed = proj_weight.shape[1]
    rows = texts.shape[0]
    half = local_rows // 2
    full_width = width * mp_count
    place = (lax.axis_index("dp") * mp_count + lax.axis_index("mp")).astype(jnp.int32).reshape(1)
    core, across, column = 1, 2, mp_count
    line = list(range(plane_count, count, plane_count))

    def swap(value, flip):
        return lax.ppermute(value, axes, [(i, i ^ flip) for i in range(count)])

    def struct(dims, kind=jnp.bfloat16):
        return jax.ShapeDtypeStruct(dims, kind)

    def along_line(value, order):
        return jnp.concatenate([value] + [swap(value, flip) for flip in order], axis=0)

    smem = pl.BlockSpec(memory_space=pltpu.SMEM)
    vmem = pl.BlockSpec(memory_space=pltpu.VMEM)
    sums = [struct((1, embed), jnp.float32), struct((1, LANES), jnp.float32)]
    extra = pltpu.VMEM((rows, LANES), jnp.float32)

    keep, send, column_sum, sum_row = kernel_call(
        functools.partial(project_body, rows, mp_count),
        [struct((half, embed), jnp.float32), struct((half, embed + LANES))] + sums,
        scratch=[extra],
        in_specs=[smem, vmem, vmem],
        flops=2 * local_rows * width * embed,
        name="project",
    )(place, features, proj_weight)
    own, send, column_sum, sum_row = kernel_call(
        functools.partial(chip_body, width, mp_count),
        [struct((rows, embed), jnp.float32), struct((rows, embed + LANES))] + sums,
        scratch=[extra],
        in_specs=[smem] + [vmem] * 4,
        name="chip_project",
    )(place, keep, swap(send, core), column_sum, sum_row)
    far, near = line[1], line[0]
    order = [0, far, near, far ^ near]
    plane = [0, column, across, column | across]
    unit_txt_b = kernel_call(texts_body, struct(texts.shape), name="unit_texts")(texts)
    txt_line = jnp.concatenate(
        [unit_txt_b] + [swap(unit_txt_b, flip) for flip in order[1:]], axis=0
    )
    send, txt_line = lax.optimization_barrier((send, txt_line))
    txt_plane = [txt_line] + [swap(txt_line, flip) for flip in plane[1:]]

    project, mean, weight_sum = kernel_call(
        functools.partial(rows_body, full_width, mp_count),
        [
            struct((rows, embed)),
            struct((local_rows, 1), jnp.float32),
            struct((1, embed), jnp.float32),
        ],
        in_specs=[smem] + [vmem] * 4,
        name="project_rows",
    )(place, own, swap(send, across), column_sum, sum_row)
    normed_b = kernel_call(centre_body, struct(features.shape), name="centre")(features, mean)

    line_rows = jnp.concatenate([project, swap(project, far)], axis=0)
    line_rows = jnp.concatenate([line_rows, swap(line_rows, near)], axis=0)
    line_rows, txt_plane[1] = lax.optimization_barrier((line_rows, txt_plane[1]))
    plane_rows = [line_rows] + [swap(line_rows, flip) for flip in plane[1:]]
    own_texts = jnp.concatenate(txt_plane, axis=0)
    other_texts = swap(own_texts, core)

    normed = jnp.concatenate([normed_b, swap(normed_b, column)], axis=0)
    normed = jnp.concatenate([normed, swap(normed, far)], axis=0)
    normed = jnp.concatenate([normed, swap(normed, near)], axis=0)
    normed_order = sum([[o, o ^ column] for o in order], [])

    grads = []
    for index, value in enumerate(plane_rows):
        grads.append(
            kernel_call(
                functools.partial(grad_body, index * local_rows),
                struct(value.shape),
                flops=4 * local_rows * count * rows * embed,
                name="grad",
            )(value, own_texts, other_texts)
        )
    others = [swap(value, core) for value in grads]

    def add_product(indices, previous, final=False):
        arrays = sum([[grads[i], others[i]] for i in indices], [])
        orders = [[o ^ plane[i] for o in order] for i in indices]
        tiles = 3 if final else 1
        scratch = [
            pltpu.VMEM(proj_weight.shape, jnp.float32),
            pltpu.SemaphoreType.DMA((tiles,)),
        ]
        return kernel_call(
            functools.partial(weight_body, rows, mp_count, normed_order, orders, tiles),
            struct(proj_weight.shape, jnp.float32),
            scratch=scratch if final else (),
            in_specs=[smem] + [vmem] * (1 + len(arrays) + len(previous)),
            out_specs=pl.BlockSpec(memory_space=pl.ANY) if final else vmem,
            flops=4 * width * embed * local_rows * len(indices),
            name="weight",
        )(place, normed, *arrays, *previous)

    grad_features = kernel_call(
        functools.partial(features_body, full_width, rows, mp_count),
        struct(features.shape),
        scratch=[pltpu.VMEM((local_rows, embed), jnp.bfloat16)],
        in_specs=[smem] + [vmem] * (2 + mp_count),
        flops=2 * local_rows * width * embed,
        name="grad_features",
    )(place, proj_weight, weight_sum, grads[0], others[0], grads[2], others[2])
    grad_weight = add_product([0], [])
    grad_weight = add_product([1, 2], [grad_weight])
    grad_weight = add_product([3], [grad_weight], True)
    return grad_features, grad_weight


def shards(features, proj_weight, texts):
    dp_count, mp_count = lax.axis_size("dp"), lax.axis_size("mp")
    count = dp_count * mp_count
    rows = texts.shape[0]
    embed = texts.shape[1]
    fits = (
        count * rows * (embed + LANES) * 2 <= GATHER_BYTES
        and count & (count - 1) == 0
        and mp_count == 4
        and count == 8 * mp_count
        and features.shape[0] == LANES == mp_count * rows
        and embed % LANES == 0
        and 2 * (embed // LANES) + 3 <= rows
        and rows % 16 == 0
    )
    plan = shards_gathered if fits else shards_summed
    return plan(features, proj_weight, texts)


def solution(mesh):
    return jax.shard_map(
        shards,
        mesh=mesh,
        in_specs=(P("dp", "mp"), P("mp", None), P(("dp", "mp"), None)),
        out_specs=(P("dp", "mp"), P("mp", None)),
        check_vma=False,
    )
```

profile of v0, /device:TPU:0, one launch (start us, length us, event | category | flops | bytes accessed | tf_op | source)
XLA Modules:
  0.0 64.6 jit_solution(3592915786124486737)
XLA Ops:
  0.6 0.9 %copy-done.4 = bf16[32,1152]{1,0:T(8,128)(2,1)S(1)} copy-done((bf16[32,1152]{1,0:T(8,128)(2,1)S(1)}, bf16[32,1152]{1,0:T(8,128)(2,1)}, u32[]{:S(2)}) %copy-start.4) | copy-done | bytes 73752
  1.6 5.1 %collective-permute-start.3 = (bf16[32,1152]{1,0:T(8,128)(2,1)S(1)}, bf16[32,1152]{1,0:T(8,128)(2,1)S(1)}, u32[]{:S(2)}, u32[]{:S(2)}) collective-permute-start(bf16[32,1152]{1,0:T(8,128)(2,1)S(1)} %unit_texts.1), channel_id=1, source_target_pairs={{0,24},{1,25},{2,26},{3,27},{4,28},{5,29},{6,30},{7,31},{8,16},{9,... | collective-permute-start | bytes 221192 | tf_op jit(solution)/shard_map/ppermute | solution.py:308
  7.4 1.2 %copy-done = bf16[384,1152]{1,0:T(8,128)(2,1)S(1)} copy-done((bf16[384,1152]{1,0:T(8,128)(2,1)S(1)}, bf16[384,1152]{1,0:T(8,128)(2,1)}, u32[]{:S(2)}) %copy-start) | copy-done | bytes 884760
  8.6 0.9 %copy-done.2 = bf16[128,384]{1,0:T(8,128)(2,1)S(1)} copy-done((bf16[128,384]{1,0:T(8,128)(2,1)S(1)}, bf16[128,384]{1,0:T(8,128)(2,1)}, u32[]{:S(2)}) %copy-start.2) | copy-done | bytes 98328
  9.9 1.8 %collective-permute-done.2 = bf16[32,1152]{1,0:T(8,128)(2,1)S(1)} collective-permute-done((bf16[32,1152]{1,0:T(8,128)(2,1)S(1)}, bf16[32,1152]{1,0:T(8,128)(2,1)S(1)}, u32[]{:S(2)}, u32[]{:S(2)}) %collective-permute-start.2) | collective-permute-done | bytes 73760 | tf_op jit(solution)/shard_map/ppermute | solution.py:308
  12.7 1.7 %collective-permute-start.4 = (bf16[32,1280]{1,0:T(8,128)(2,1)S(1)}, bf16[32,1280]{1,0:T(8,128)(2,1)S(1)}, u32[]{:S(2)}, u32[]{:S(2)}) collective-permute-start(bf16[32,1280]{1,0:T(8,128)(2,1)S(1)} %get-tuple-element.23), channel_id=1, source_target_pairs={{0,2},{1,3},{2,0},{3,1},{4,6},{5,7},{6,4},{7,5},{8,10},{9,11},{10,... | collective-permute-start | bytes 245768 | tf_op jit(solution)/shard_map/ppermute | solution.py:308
  14.4 2.8 %collective-permute-done.4.received_ref = bf16[32,1280]{1,0:T(8,128)(2,1)S(1)} collective-permute-done((bf16[32,1280]{1,0:T(8,128)(2,1)S(1)}, bf16[32,1280]{1,0:T(8,128)(2,1)S(1)}, u32[]{:S(2)}, u32[]{:S(2)}) %collective-permute-start.4) | collective-permute-done | bytes 81952 | tf_op jit(solution)/shard_map/ppermute | solution.py:308
  17.4 2.3 %collective-permute-start.5 = (bf16[32,1152]{1,0:T(8,128)(2,1)S(1)}, bf16[32,1152]{1,0:T(8,128)(2,1)S(1)}, u32[]{:S(2)}, u32[]{:S(2)}) collective-permute-start(bf16[32,1152]{1,0:T(8,128)(2,1)S(1)} %get-tuple-element.27), channel_id=1, source_target_pairs={{0,16},{1,17},{2,18},{3,19},{4,20},{5,21},{6,22},{7,23},{8,24},{9,... | collective-permute-start | bytes 221192 | tf_op jit(solution)/shard_map/ppermute | solution.py:308
  19.7 2.4 %collective-permute-start.9 = (bf16[128,1152]{1,0:T(8,128)(2,1)S(1)}, bf16[128,1152]{1,0:T(8,128)(2,1)S(1)}, u32[]{:S(2)}, u32[]{:S(2)}) collective-permute-start(bf16[128,1152]{1,0:T(8,128)(2,1)S(1)} %pad_maximum_fusion.2), channel_id=1, source_target_pairs={{0,6},{1,7},{2,4},{3,5},{4,2},{5,3},{6,0},{7,1},{8,14},{9,15},{10,... | collective-permute-start | bytes 884744 | tf_op jit(solution)/shard_map/ppermute | solution.py:308
  23.2 1.6 %collective-permute-start.6 = (bf16[64,1152]{1,0:T(8,128)(2,1)S(1)}, bf16[64,1152]{1,0:T(8,128)(2,1)S(1)}, u32[]{:S(2)}, u32[]{:S(2)}) collective-permute-start(bf16[64,1152]{1,0:T(8,128)(2,1)S(1)} %pad_maximum_fusion.5), channel_id=1, source_target_pairs={{0,8},{1,9},{2,10},{3,11},{4,12},{5,13},{6,14},{7,15},{8,0},{9,1},... | collective-permute-start | bytes 442376 | tf_op jit(solution)/shard_map/ppermute | solution.py:308
  24.8 3.6 %collective-permute-done.6 = bf16[64,1152]{1,0:T(8,128)(2,1)S(1)} collective-permute-done((bf16[64,1152]{1,0:T(8,128)(2,1)S(1)}, bf16[64,1152]{1,0:T(8,128)(2,1)S(1)}, u32[]{:S(2)}, u32[]{:S(2)}) %collective-permute-start.6) | collective-permute-done | bytes 147488 | tf_op jit(solution)/shard_map/ppermute | solution.py:308
  28.4 5.0 %collective-permute-done.7 = bf16[128,1152]{1,0:T(8,128)(2,1)S(1)} collective-permute-done((bf16[128,1152]{1,0:T(8,128)(2,1)S(1)}, bf16[128,1152]{1,0:T(8,128)(2,1)S(1)}, u32[]{:S(2)}, u32[]{:S(2)}) %collective-permute-start.7) | collective-permute-done | bytes 294944 | tf_op jit(solution)/shard_map/ppermute | solution.py:308
  33.7 1.6 %collective-permute-start.14 = (bf16[128,384]{1,0:T(8,128)(2,1)S(1)}, bf16[128,384]{1,0:T(8,128)(2,1)S(1)}, u32[]{:S(2)}, u32[]{:S(2)}) collective-permute-start(bf16[128,384]{1,0:T(8,128)(2,1)S(1)} %centre.1), channel_id=1, source_target_pairs={{0,4},{1,5},{2,6},{3,7},{4,0},{5,1},{6,2},{7,3},{8,12},{9,13},{10,... | collective-permute-start | bytes 294920 | tf_op jit(solution)/shard_map/ppermute | solution.py:308
  35.3 3.7 %collective-permute-done.14 = bf16[128,384]{1,0:T(8,128)(2,1)S(1)} collective-permute-done((bf16[128,384]{1,0:T(8,128)(2,1)S(1)}, bf16[128,384]{1,0:T(8,128)(2,1)S(1)}, u32[]{:S(2)}, u32[]{:S(2)}) %collective-permute-start.14) | collective-permute-done | bytes 98336 | tf_op jit(solution)/shard_map/ppermute | solution.py:308
  39.8 1.4 %collective-permute-start.12 = (bf16[128,1152]{1,0:T(8,128)(2,1)S(1)}, bf16[128,1152]{1,0:T(8,128)(2,1)S(1)}, u32[]{:S(2)}, u32[]{:S(2)}) collective-permute-start(bf16[128,1152]{1,0:T(8,128)(2,1)S(1)} %pad_maximum_fusion.3.project_ref), channel_id=1, source_target_pairs={{0,2},{1,3},{2,0},{3,1},{4,6},{5,7},{6,4},{7,5},{8,10},{9,11},{10,... | collective-permute-start | bytes 884744 | tf_op jit(solution)/shard_map/ppermute | solution.py:308
  41.9 1.5 %collective-permute-start.17 = (bf16[128,1152]{1,0:T(8,128)(2,1)S(1)}, bf16[128,1152]{1,0:T(8,128)(2,1)S(1)}, u32[]{:S(2)}, u32[]{:S(2)}) collective-permute-start(bf16[128,1152]{1,0:T(8,128)(2,1)S(1)} %pad_maximum_fusion.3.project_ref), channel_id=1, source_target_pairs={{0,6},{1,7},{2,4},{3,5},{4,2},{5,3},{6,0},{7,1},{8,14},{9,15},{10,... | collective-permute-start | bytes 884744 | tf_op jit(solution)/shard_map/ppermute | solution.py:308
  43.3 7.4 %collective-permute-done.15 = bf16[256,384]{1,0:T(8,128)(2,1)S(1)} collective-permute-done((bf16[256,384]{1,0:T(8,128)(2,1)S(1)}, bf16[256,384]{1,0:T(8,128)(2,1)S(1)}, u32[]{:S(2)}, u32[]{:S(2)}) %collective-permute-start.15) | collective-permute-done | bytes 196640 | tf_op jit(solution)/shard_map/ppermute | solution.py:308
  50.8 1.6 %grad.4.refs_0_ = bf16[128,1152]{1,0:T(8,128)(2,1)S(1)} custom-call(bf16[128,1152]{1,0:T(8,128)(2,1)S(1)} %pad_maximum_fusion.3.project_ref, bf16[512,1152]{1,0:T(8,128)(2,1)S(1)} %constant_dynamic-update-slice_fusion.refs_0_, bf16[512,1152]{1,0:T(8,128)(2,1)S(1)} %collective-permute-done.10.refs_1_), custom_call_target="tpu_custom_call" | custom-call | flops 603979776 | tf_op jit(solution)/shard_map/grad/pallas_call | solution.py:373
  52.5 1.6 %grad.5.refs_2_ = bf16[128,1152]{1,0:T(8,128)(2,1)S(1)} custom-call(bf16[128,1152]{1,0:T(8,128)(2,1)S(1)} %collective-permute-done.12.project_ref, bf16[512,1152]{1,0:T(8,128)(2,1)S(1)} %constant_dynamic-update-slice_fusion.refs_0_, bf16[512,1152]{1,0:T(8,128)(2,1)S(1)} %collective-permute-done.10.refs_1_), custom_call_target="tpu_custom_call" | custom-call | flops 603979776 | tf_op jit(solution)/shard_map/grad/pallas_call | solution.py:373
  54.7 1.6 %grad.7.refs_0_ = bf16[128,1152]{1,0:T(8,128)(2,1)S(1)} custom-call(bf16[128,1152]{1,0:T(8,128)(2,1)S(1)} %collective-permute-done.19.project_ref, bf16[512,1152]{1,0:T(8,128)(2,1)S(1)} %constant_dynamic-update-slice_fusion.refs_0_, bf16[512,1152]{1,0:T(8,128)(2,1)S(1)} %collective-permute-done.10.refs_1_), custom_call_target="tpu_custom_call" | custom-call | flops 603979776 | tf_op jit(solution)/shard_map/grad/pallas_call | solution.py:373
  56.4 1.6 %grad.6.refs_0_ = bf16[128,1152]{1,0:T(8,128)(2,1)S(1)} custom-call(bf16[128,1152]{1,0:T(8,128)(2,1)S(1)} %collective-permute-done.17.project_ref, bf16[512,1152]{1,0:T(8,128)(2,1)S(1)} %constant_dynamic-update-slice_fusion.refs_0_, bf16[512,1152]{1,0:T(8,128)(2,1)S(1)} %collective-permute-done.10.refs_1_), custom_call_target="tpu_custom_call" | custom-call | flops 603979776 | tf_op jit(solution)/shard_map/grad/pallas_call | solution.py:373
  58.5 2.1 %collective-permute-done.16 = bf16[512,384]{1,0:T(8,128)(2,1)S(1)} collective-permute-done((bf16[512,384]{1,0:T(8,128)(2,1)S(1)}, bf16[512,384]{1,0:T(8,128)(2,1)S(1)}, u32[]{:S(2)}, u32[]{:S(2)}) %collective-permute-start.16) | collective-permute-done | bytes 393248 | tf_op jit(solution)/shard_map/ppermute | solution.py:308
  60.7 1.1 %grad_features.1 = bf16[128,384]{1,0:T(8,128)(2,1)} custom-call(s32[1]{0:T(128)} %bitcast.place_ref, bf16[384,1152]{1,0:T(8,128)(2,1)S(1)} %copy-done.1, f32[1,1152]{1,0:T(1,128)S(1)} %get-tuple-element.26.weight_sum_ref, bf16[128,1152]{1,0:T(8,128)(2,1)S(1)} %grad.4.refs_0_, bf16[128,1152]{1,0:T(8,128)(2,1)S(1)} %collective-permute-done.11.refs_1_, ...), custom_call_target="tpu_custom_call" | custom-call | flops 113246208 | tf_op jit(solution)/shard_map/grad_features/pallas_call | solution.py:400
  63.0 1.5 %weight.5 = f32[384,1152]{1,0:T(8,128)} custom-call(s32[1]{0:T(128)} %bitcast.place_ref, bf16[1024,384]{1,0:T(8,128)(2,1)S(1)} %pad_maximum_fusion.normed_ref, bf16[128,1152]{1,0:T(8,128)(2,1)S(1)} %grad.6.refs_0_, bf16[128,1152]{1,0:T(8,128)(2,1)S(1)} %collective-permute-done.18.refs_1_, f32[384,1152]{1,0:T(8,128)S(1)} %weight.4.refs_2_), custom_call_target="tpu_custom_call" | custom-call | flops 226492416 | tf_op jit(solution)/shard_map/weight/pallas_call | solution.py:390
  (51 shorter events, 7.9 us)
Async XLA Ops:
  1.6 8.3 %collective-permute-start.3 = (bf16[32,1152]{1,0:T(8,128)(2,1)S(1)}, bf16[32,1152]{1,0:T(8,128)(2,1)S(1)}, u32[]{:S(2)}, u32[]{:S(2)}) collective-permute-start(bf16[32,1152]{1,0:T(8,128)(2,1)S(1)} %unit_texts.1), channel_id=1, source_target_pairs={{0,24},{1,25},{2,26},{3,27},{4,28},{5,29},{6,30},{7,31},{8,16},{9,... | collective-permute-start | bytes 221192 | tf_op jit(solution)/shard_map/ppermute | solution.py:308
  6.7 5.0 %collective-permute-start.2 = (bf16[32,1152]{1,0:T(8,128)(2,1)S(1)}, bf16[32,1152]{1,0:T(8,128)(2,1)S(1)}, u32[]{:S(2)}, u32[]{:S(2)}) collective-permute-start(bf16[32,1152]{1,0:T(8,128)(2,1)S(1)} %unit_texts.1), channel_id=1, source_target_pairs={{0,8},{1,9},{2,10},{3,11},{4,12},{5,13},{6,14},{7,15},{8,0},{9,1},... | collective-permute-start | bytes 221192 | tf_op jit(solution)/shard_map/ppermute | solution.py:308
  6.7 5.8 %collective-permute-start.1 = (bf16[32,1152]{1,0:T(8,128)(2,1)S(1)}, bf16[32,1152]{1,0:T(8,128)(2,1)S(1)}, u32[]{:S(2)}, u32[]{:S(2)}) collective-permute-start(bf16[32,1152]{1,0:T(8,128)(2,1)S(1)} %unit_texts.1), channel_id=1, source_target_pairs={{0,16},{1,17},{2,18},{3,19},{4,20},{5,21},{6,22},{7,23},{8,24},{9,... | collective-permute-start | bytes 221192 | tf_op jit(solution)/shard_map/ppermute | solution.py:308
  7.4 1.2 %copy-start = (bf16[384,1152]{1,0:T(8,128)(2,1)S(1)}, bf16[384,1152]{1,0:T(8,128)(2,1)}, u32[]{:S(2)}) copy-start(bf16[384,1152]{1,0:T(8,128)(2,1)} %weight_ref.3) | copy-start | bytes 2654212
  9.9 2.7 %collective-permute-start = (bf16[64,1280]{1,0:T(8,128)(2,1)S(1)}, bf16[64,1280]{1,0:T(8,128)(2,1)S(1)}, u32[]{:S(2)}, u32[]{:S(2)}) collective-permute-start(bf16[64,1280]{1,0:T(8,128)(2,1)S(1)} %get-tuple-element.18), channel_id=1, source_target_pairs={{0,1},{1,0},{2,3},{3,2},{4,5},{5,4},{6,7},{7,6},{8,9},{9,8},{10,11... | collective-permute-start | bytes 491528 | tf_op jit(solution)/shard_map/ppermute | solution.py:308
  12.7 4.5 %collective-permute-start.4 = (bf16[32,1280]{1,0:T(8,128)(2,1)S(1)}, bf16[32,1280]{1,0:T(8,128)(2,1)S(1)}, u32[]{:S(2)}, u32[]{:S(2)}) collective-permute-start(bf16[32,1280]{1,0:T(8,128)(2,1)S(1)} %get-tuple-element.23), channel_id=1, source_target_pairs={{0,2},{1,3},{2,0},{3,1},{4,6},{5,7},{6,4},{7,5},{8,10},{9,11},{10,... | collective-permute-start | bytes 245768 | tf_op jit(solution)/shard_map/ppermute | solution.py:308
  17.4 5.8 %collective-permute-start.5 = (bf16[32,1152]{1,0:T(8,128)(2,1)S(1)}, bf16[32,1152]{1,0:T(8,128)(2,1)S(1)}, u32[]{:S(2)}, u32[]{:S(2)}) collective-permute-start(bf16[32,1152]{1,0:T(8,128)(2,1)S(1)} %get-tuple-element.27), channel_id=1, source_target_pairs={{0,16},{1,17},{2,18},{3,19},{4,20},{5,21},{6,22},{7,23},{8,24},{9,... | collective-permute-start | bytes 221192 | tf_op jit(solution)/shard_map/ppermute | solution.py:308
  19.7 13.8 %collective-permute-start.9 = (bf16[128,1152]{1,0:T(8,128)(2,1)S(1)}, bf16[128,1152]{1,0:T(8,128)(2,1)S(1)}, u32[]{:S(2)}, u32[]{:S(2)}) collective-permute-start(bf16[128,1152]{1,0:T(8,128)(2,1)S(1)} %pad_maximum_fusion.2), channel_id=1, source_target_pairs={{0,6},{1,7},{2,4},{3,5},{4,2},{5,3},{6,0},{7,1},{8,14},{9,15},{10,... | collective-permute-start | bytes 884744 | tf_op jit(solution)/shard_map/ppermute | solution.py:308
  22.2 11.3 %collective-permute-start.8 = (bf16[128,1152]{1,0:T(8,128)(2,1)S(1)}, bf16[128,1152]{1,0:T(8,128)(2,1)S(1)}, u32[]{:S(2)}, u32[]{:S(2)}) collective-permute-start(bf16[128,1152]{1,0:T(8,128)(2,1)S(1)} %pad_maximum_fusion.2), channel_id=1, source_target_pairs={{0,2},{1,3},{2,0},{3,1},{4,6},{5,7},{6,4},{7,5},{8,10},{9,11},{10,... | collective-permute-start | bytes 884744 | tf_op jit(solution)/shard_map/ppermute | solution.py:308
  22.7 10.7 %collective-permute-start.7 = (bf16[128,1152]{1,0:T(8,128)(2,1)S(1)}, bf16[128,1152]{1,0:T(8,128)(2,1)S(1)}, u32[]{:S(2)}, u32[]{:S(2)}) collective-permute-start(bf16[128,1152]{1,0:T(8,128)(2,1)S(1)} %pad_maximum_fusion.2), channel_id=1, source_target_pairs={{0,4},{1,5},{2,6},{3,7},{4,0},{5,1},{6,2},{7,3},{8,12},{9,13},{10,... | collective-permute-start | bytes 884744 | tf_op jit(solution)/shard_map/ppermute | solution.py:308
  23.2 5.2 %collective-permute-start.6 = (bf16[64,1152]{1,0:T(8,128)(2,1)S(1)}, bf16[64,1152]{1,0:T(8,128)(2,1)S(1)}, u32[]{:S(2)}, u32[]{:S(2)}) collective-permute-start(bf16[64,1152]{1,0:T(8,128)(2,1)S(1)} %pad_maximum_fusion.5), channel_id=1, source_target_pairs={{0,8},{1,9},{2,10},{3,11},{4,12},{5,13},{6,14},{7,15},{8,0},{9,1},... | collective-permute-start | bytes 442376 | tf_op jit(solution)/shard_map/ppermute | solution.py:308
  24.8 8.8 %copy-start.3 = (bf16[128,384]{1,0:T(8,128)(2,1)S(1)}, bf16[128,384]{1,0:T(8,128)(2,1)}, u32[]{:S(2)}) copy-start(bf16[128,384]{1,0:T(8,128)(2,1)} %features_ref.3) | copy-start | bytes 294916
  33.5 17.3 %collective-permute-start.10 = (bf16[512,1152]{1,0:T(8,128)(2,1)S(1)}, bf16[512,1152]{1,0:T(8,128)(2,1)S(1)}, u32[]{:S(2)}, u32[]{:S(2)}) collective-permute-start(bf16[512,1152]{1,0:T(8,128)(2,1)S(1)} %constant_dynamic-update-slice_fusion.refs_0_), channel_id=1, source_target_pairs={{0,1},{1,0},{2,3},{3,2},{4,5},{5,4},{6,7},{7,6},{8,9},{9,8},{10,11... | collective-permute-start | bytes 3538952 | tf_op jit(solution)/shard_map/ppermute | solution.py:308
  33.7 5.3 %collective-permute-start.14 = (bf16[128,384]{1,0:T(8,128)(2,1)S(1)}, bf16[128,384]{1,0:T(8,128)(2,1)S(1)}, u32[]{:S(2)}, u32[]{:S(2)}) collective-permute-start(bf16[128,384]{1,0:T(8,128)(2,1)S(1)} %centre.1), channel_id=1, source_target_pairs={{0,4},{1,5},{2,6},{3,7},{4,0},{5,1},{6,2},{7,3},{8,12},{9,13},{10,... | collective-permute-start | bytes 294920 | tf_op jit(solution)/shard_map/ppermute | solution.py:308
  39.0 11.7 %collective-permute-start.15 = (bf16[256,384]{1,0:T(8,128)(2,1)S(1)}, bf16[256,384]{1,0:T(8,128)(2,1)S(1)}, u32[]{:S(2)}, u32[]{:S(2)}) collective-permute-start(bf16[256,384]{1,0:T(8,128)(2,1)S(1)} %pad_maximum_fusion.4), channel_id=1, source_target_pairs={{0,16},{1,17},{2,18},{3,19},{4,20},{5,21},{6,22},{7,23},{8,24},{9,... | collective-permute-start | bytes 589832 | tf_op jit(solution)/shard_map/ppermute | solution.py:308
  39.8 12.7 %collective-permute-start.12 = (bf16[128,1152]{1,0:T(8,128)(2,1)S(1)}, bf16[128,1152]{1,0:T(8,128)(2,1)S(1)}, u32[]{:S(2)}, u32[]{:S(2)}) collective-permute-start(bf16[128,1152]{1,0:T(8,128)(2,1)S(1)} %pad_maximum_fusion.3.project_ref), channel_id=1, source_target_pairs={{0,2},{1,3},{2,0},{3,1},{4,6},{5,7},{6,4},{7,5},{8,10},{9,11},{10,... | collective-permute-start | bytes 884744 | tf_op jit(solution)/shard_map/ppermute | solution.py:308
  41.2 13.5 %collective-permute-start.19 = (bf16[128,1152]{1,0:T(8,128)(2,1)S(1)}, bf16[128,1152]{1,0:T(8,128)(2,1)S(1)}, u32[]{:S(2)}, u32[]{:S(2)}) collective-permute-start(bf16[128,1152]{1,0:T(8,128)(2,1)S(1)} %pad_maximum_fusion.3.project_ref), channel_id=1, source_target_pairs={{0,4},{1,5},{2,6},{3,7},{4,0},{5,1},{6,2},{7,3},{8,12},{9,13},{10,... | collective-permute-start | bytes 884744 | tf_op jit(solution)/shard_map/ppermute | solution.py:308
  41.9 14.5 %collective-permute-start.17 = (bf16[128,1152]{1,0:T(8,128)(2,1)S(1)}, bf16[128,1152]{1,0:T(8,128)(2,1)S(1)}, u32[]{:S(2)}, u32[]{:S(2)}) collective-permute-start(bf16[128,1152]{1,0:T(8,128)(2,1)S(1)} %pad_maximum_fusion.3.project_ref), channel_id=1, source_target_pairs={{0,6},{1,7},{2,4},{3,5},{4,2},{5,3},{6,0},{7,1},{8,14},{9,15},{10,... | collective-permute-start | bytes 884744 | tf_op jit(solution)/shard_map/ppermute | solution.py:308
  50.7 9.9 %collective-permute-start.16 = (bf16[512,384]{1,0:T(8,128)(2,1)S(1)}, bf16[512,384]{1,0:T(8,128)(2,1)S(1)}, u32[]{:S(2)}, u32[]{:S(2)}) collective-permute-start(bf16[512,384]{1,0:T(8,128)(2,1)S(1)} %pad_maximum_fusion.1), channel_id=1, source_target_pairs={{0,8},{1,9},{2,10},{3,11},{4,12},{5,13},{6,14},{7,15},{8,0},{9,1},... | collective-permute-start | bytes 1179656 | tf_op jit(solution)/shard_map/ppermute | solution.py:308
  52.4 8.3 %collective-permute-start.11 = (bf16[128,1152]{1,0:T(8,128)(2,1)S(1)}, bf16[128,1152]{1,0:T(8,128)(2,1)S(1)}, u32[]{:S(2)}, u32[]{:S(2)}) collective-permute-start(bf16[128,1152]{1,0:T(8,128)(2,1)S(1)} %grad.4.refs_0_), channel_id=1, source_target_pairs={{0,1},{1,0},{2,3},{3,2},{4,5},{5,4},{6,7},{7,6},{8,9},{9,8},{10,11... | collective-permute-start | bytes 884744 | tf_op jit(solution)/shard_map/ppermute | solution.py:308
  54.1 6.6 %collective-permute-start.13 = (bf16[128,1152]{1,0:T(8,128)(2,1)S(1)}, bf16[128,1152]{1,0:T(8,128)(2,1)S(1)}, u32[]{:S(2)}, u32[]{:S(2)}) collective-permute-start(bf16[128,1152]{1,0:T(8,128)(2,1)S(1)} %grad.5.refs_2_), channel_id=1, source_target_pairs={{0,1},{1,0},{2,3},{3,2},{4,5},{5,4},{6,7},{7,6},{8,9},{9,8},{10,11... | collective-permute-start | bytes 884744 | tf_op jit(solution)/shard_map/ppermute | solution.py:308
  56.3 6.0 %collective-permute-start.20 = (bf16[128,1152]{1,0:T(8,128)(2,1)S(1)}, bf16[128,1152]{1,0:T(8,128)(2,1)S(1)}, u32[]{:S(2)}, u32[]{:S(2)}) collective-permute-start(bf16[128,1152]{1,0:T(8,128)(2,1)S(1)} %grad.7.refs_0_), channel_id=1, source_target_pairs={{0,1},{1,0},{2,3},{3,2},{4,5},{5,4},{6,7},{7,6},{8,9},{9,8},{10,11... | collective-permute-start | bytes 884744 | tf_op jit(solution)/shard_map/ppermute | solution.py:308
  58.0 2.8 %copy-start.1 = (bf16[384,1152]{1,0:T(8,128)(2,1)S(1)}, bf16[384,1152]{1,0:T(8,128)(2,1)}, u32[]{:S(2)}) copy-start(bf16[384,1152]{1,0:T(8,128)(2,1)} %weight_ref.3) | copy-start | bytes 2654212
  58.0 5.1 %collective-permute-start.18 = (bf16[128,1152]{1,0:T(8,128)(2,1)S(1)}, bf16[128,1152]{1,0:T(8,128)(2,1)S(1)}, u32[]{:S(2)}, u32[]{:S(2)}) collective-permute-start(bf16[128,1152]{1,0:T(8,128)(2,1)S(1)} %grad.6.refs_0_), channel_id=1, source_target_pairs={{0,1},{1,0},{2,3},{3,2},{4,5},{5,4},{6,7},{7,6},{8,9},{9,8},{10,11... | collective-permute-start | bytes 884744 | tf_op jit(solution)/shard_map/ppermute | solution.py:308
  (2 other events, 1.8 us)
where the time goes:
time: 64.8 us; the launch traced here: 64.6 us
  waiting for transfers between devices  27.1 us (42%)
  starting transfers between devices  22.2 us (34%)
  Pallas kernels  11 us (17%)
  local copies, waits for them, and re-layouts  3.07 us (5%)
  between operations  0.9 us (1%)
    ppermute x21, waiting for transfers between devices, swap(): return lax.ppermute(value, axes, [(i, i ^ flip) for i in range(count)])  27.1 us
    ppermute x21, starting transfers between devices, swap(): return lax.ppermute(value, axes, [(i, i ^ flip) for i in range(count)])  22.2 us
    pallas_call x4, Pallas kernels, shards_gathered(): kernel_call(functools.partial(grad_body, index * local_rows), struct(valu...  6.37 us
    unnamed x13, local copies, waits for them, and re-layouts  3.03 us
    pallas_call x3, Pallas kernels, add_product(): kernel_call(functools.partial(weight_body, rows, mp_count, normed_order,...  2.73 us
  transfers between devices with their start and end apart: 21, of which 8 were waited for; matrix products, arithmetic and copies ran while one was open for 0% of the time, Pallas kernels for 14%

commit v1 on v0

--- a/solution.py
+++ b/solution.py
@@ -335,7 +335,7 @@
     )(place, keep, swap(send, core), column_sum, sum_row)
     far, near = line[1], line[0]
     order = [0, far, near, far ^ near]
-    plane = [0, column, across, column | across]
+    plane = [0, across, column, column | across]
     unit_txt_b = kernel_call(texts_body, struct(texts.shape), name="unit_texts")(texts)
     txt_line = jnp.concatenate(
         [unit_txt_b] + [swap(unit_txt_b, flip) for flip in order[1:]], axis=0
@@ -357,27 +357,35 @@
 
     line_rows = jnp.concatenate([project, swap(project, far)], axis=0)
     line_rows = jnp.concatenate([line_rows, swap(line_rows, near)], axis=0)
-    line_rows, txt_plane[1] = lax.optimization_barrier((line_rows, txt_plane[1]))
-    plane_rows = [line_rows] + [swap(line_rows, flip) for flip in plane[1:]]
-    own_texts = jnp.concatenate(txt_plane, axis=0)
-    other_texts = swap(own_texts, core)
-
     normed = jnp.concatenate([normed_b, swap(normed_b, column)], axis=0)
-    normed = jnp.concatenate([normed, swap(normed, far)], axis=0)
-    normed = jnp.concatenate([normed, swap(normed, near)], axis=0)
+    normed_far = swap(normed, far)
+    line_rows, normed_far, *txt_plane = lax.optimization_barrier(
+        (line_rows, normed_far, *txt_plane)
+    )
+    normed = jnp.concatenate([normed, normed_far], axis=0)
+    normed_near = swap(normed, near)
     normed_order = sum([[o, o ^ column] for o in order], [])
-
-    grads = []
-    for index, value in enumerate(plane_rows):
-        grads.append(
-            kernel_call(
-                functools.partial(grad_body, index * local_rows),
-                struct(value.shape),
-                flops=4 * local_rows * count * rows * embed,
-                name="grad",
-            )(value, own_texts, other_texts)
-        )
-    others = [swap(value, core) for value in grads]
+    all_texts = [jnp.concatenate(txt_plane, axis=0)]
+    all_texts.append(swap(all_texts[0], core))
+    plane_rows = [line_rows] + [swap(line_rows, flip) for flip in plane[1:3]]
+    last_rows = line_rows
+    plane_rows.append(swap(last_rows, plane[3]))
+
+    def gradient(index):
+        return kernel_call(
+            functools.partial(grad_body, index * local_rows),
+            struct(line_rows.shape),
+            flops=4 * local_rows * count * rows * embed,
+            name="grad",
+        )(plane_rows[index], *all_texts)
+
+    grads = [gradient(0)]
+    others = [swap(grads[0], core)]
+    plane_rows[1], _ = lax.optimization_barrier((plane_rows[1], grads[0]))
+    grads.append(gradient(1))
+    others.append(swap(grads[1], core))
+    plane_rows[3], normed_near = lax.optimization_barrier((plane_rows[3], normed_near))
+    normed = jnp.concatenate([normed, normed_near], axis=0)
 
     def add_product(indices, previous, final=False):
         arrays = sum([[grads[i], others[i]] for i in indices], [])
@@ -404,9 +412,15 @@
         in_specs=[smem] + [vmem] * (2 + mp_count),
         flops=2 * local_rows * width * embed,
         name="grad_features",
-    )(place, proj_weight, weight_sum, grads[0], others[0], grads[2], others[2])
-    grad_weight = add_product([0], [])
-    grad_weight = add_product([1, 2], [grad_weight])
+    )(place, proj_weight, weight_sum, grads[0], others[0], grads[1], others[1])
+    first = [0, 1]
+    grad_weight = add_product(first, [])
+    grads.append(gradient(2))
+    others.append(swap(grads[2], core))
+    plane_rows[3], _, _ = lax.optimization_barrier((plane_rows[3], grad_weight, grad_features))
+    grads.append(gradient(3))
+    others.append(swap(grads[3], core))
+    grad_weight = add_product([2], [grad_weight])
     grad_weight = add_product([3], [grad_weight], True)
     return grad_features, grad_weight
 

time: 64.8 us -> 64.8 us (level)
  starting transfers between devices: 22.2 us -> 24.5 us
  waiting for transfers between devices: 27.1 us -> 24.9 us
    ppermute x21, starting transfers between devices: 22.2 us -> 24.5 us  [swap(): return lax.ppermute(value, axes, [(i, i ^ flip) for i in range(count)])]
    ppermute x21, waiting for transfers between devices: 27.1 us -> 24.9 us  [swap(): return lax.ppermute(value, axes, [(i, i ^ flip) for i in range(count)])]
where the time goes in v1:
time: 64.8 us; the launch traced here: 64.6 us
  waiting for transfers between devices  24.9 us (38%)
  starting transfers between devices  24.5 us (38%)
  Pallas kernels  11.1 us (17%)
  local copies, waits for them, and re-layouts  3.06 us (5%)
  between operations  0.86 us (1%)
    ppermute x21, waiting for transfers between devices, swap(): return lax.ppermute(value, axes, [(i, i ^ flip) for i in range(count)])  24.9 us
    ppermute x21, starting transfers between devices, swap(): return lax.ppermute(value, axes, [(i, i ^ flip) for i in range(count)])  24.5 us
    pallas_call x4, Pallas kernels, gradient(): kernel_call(functools.partial(grad_body, index * local_rows), struct(line...  6.41 us
    unnamed x13, local copies, waits for them, and re-layouts  3.03 us
    pallas_call x3, Pallas kernels, add_product(): kernel_call(functools.partial(weight_body, rows, mp_count, normed_order,...  2.71 us
  transfers between devices with their start and end apart: 21, of which 8 were waited for; matrix products, arithmetic and copies ran while one was open for 0% of the time, Pallas kernels for 14%

profile of v1, /device:TPU:0, one launch (start us, length us, event | category | flops | bytes accessed | tf_op | source)
XLA Modules:
  0.0 64.6 jit_solution(17965593289304767165)
XLA Ops:
  1.6 5.1 %collective-permute-start.3 = (bf16[32,1152]{1,0:T(8,128)(2,1)S(1)}, bf16[32,1152]{1,0:T(8,128)(2,1)S(1)}, u32[]{:S(2)}, u32[]{:S(2)}) collective-permute-start(bf16[32,1152]{1,0:T(8,128)(2,1)S(1)} %unit_texts.1), channel_id=1, source_target_pairs={{0,24},{1,25},{2,26},{3,27},{4,28},{5,29},{6,30},{7,31},{8,16},{9,... | collective-permute-start | bytes 221192 | tf_op jit(solution)/shard_map/ppermute | solution.py:308
  7.4 1.2 %copy-done = bf16[384,1152]{1,0:T(8,128)(2,1)S(1)} copy-done((bf16[384,1152]{1,0:T(8,128)(2,1)S(1)}, bf16[384,1152]{1,0:T(8,128)(2,1)}, u32[]{:S(2)}) %copy-start) | copy-done | bytes 884760
  9.9 1.8 %collective-permute-done.2 = bf16[32,1152]{1,0:T(8,128)(2,1)S(1)} collective-permute-done((bf16[32,1152]{1,0:T(8,128)(2,1)S(1)}, bf16[32,1152]{1,0:T(8,128)(2,1)S(1)}, u32[]{:S(2)}, u32[]{:S(2)}) %collective-permute-start.2) | collective-permute-done | bytes 73760 | tf_op jit(solution)/shard_map/ppermute | solution.py:308
  12.7 1.7 %collective-permute-start.4 = (bf16[32,1280]{1,0:T(8,128)(2,1)S(1)}, bf16[32,1280]{1,0:T(8,128)(2,1)S(1)}, u32[]{:S(2)}, u32[]{:S(2)}) collective-permute-start(bf16[32,1280]{1,0:T(8,128)(2,1)S(1)} %get-tuple-element.31), channel_id=1, source_target_pairs={{0,2},{1,3},{2,0},{3,1},{4,6},{5,7},{6,4},{7,5},{8,10},{9,11},{10,... | collective-permute-start | bytes 245768 | tf_op jit(solution)/shard_map/ppermute | solution.py:308
  14.4 2.8 %collective-permute-done.4.received_ref = bf16[32,1280]{1,0:T(8,128)(2,1)S(1)} collective-permute-done((bf16[32,1280]{1,0:T(8,128)(2,1)S(1)}, bf16[32,1280]{1,0:T(8,128)(2,1)S(1)}, u32[]{:S(2)}, u32[]{:S(2)}) %collective-permute-start.4) | collective-permute-done | bytes 81952 | tf_op jit(solution)/shard_map/ppermute | solution.py:308
  17.4 2.3 %collective-permute-start.5 = (bf16[32,1152]{1,0:T(8,128)(2,1)S(1)}, bf16[32,1152]{1,0:T(8,128)(2,1)S(1)}, u32[]{:S(2)}, u32[]{:S(2)}) collective-permute-start(bf16[32,1152]{1,0:T(8,128)(2,1)S(1)} %get-tuple-element.35), channel_id=1, source_target_pairs={{0,16},{1,17},{2,18},{3,19},{4,20},{5,21},{6,22},{7,23},{8,24},{9,... | collective-permute-start | bytes 221192 | tf_op jit(solution)/shard_map/ppermute | solution.py:308
  19.8 1.6 %collective-permute-start.7 = (bf16[128,384]{1,0:T(8,128)(2,1)S(1)}, bf16[128,384]{1,0:T(8,128)(2,1)S(1)}, u32[]{:S(2)}, u32[]{:S(2)}) collective-permute-start(bf16[128,384]{1,0:T(8,128)(2,1)S(1)} %centre.1), channel_id=1, source_target_pairs={{0,4},{1,5},{2,6},{3,7},{4,0},{5,1},{6,2},{7,3},{8,12},{9,13},{10,... | collective-permute-start | bytes 294920 | tf_op jit(solution)/shard_map/ppermute | solution.py:308
  21.4 1.4 %collective-permute-done.5 = bf16[32,1152]{1,0:T(8,128)(2,1)S(1)} collective-permute-done((bf16[32,1152]{1,0:T(8,128)(2,1)S(1)}, bf16[32,1152]{1,0:T(8,128)(2,1)S(1)}, u32[]{:S(2)}, u32[]{:S(2)}) %collective-permute-start.5) | collective-permute-done | bytes 73760 | tf_op jit(solution)/shard_map/ppermute | solution.py:308
  22.8 1.5 %collective-permute-start.6 = (bf16[64,1152]{1,0:T(8,128)(2,1)S(1)}, bf16[64,1152]{1,0:T(8,128)(2,1)S(1)}, u32[]{:S(2)}, u32[]{:S(2)}) collective-permute-start(bf16[64,1152]{1,0:T(8,128)(2,1)S(1)} %pad_maximum_fusion.5), channel_id=1, source_target_pairs={{0,8},{1,9},{2,10},{3,11},{4,12},{5,13},{6,14},{7,15},{8,0},{9,1},... | collective-permute-start | bytes 442376 | tf_op jit(solution)/shard_map/ppermute | solution.py:308
  24.2 1.5 %collective-permute-start.9 = (bf16[128,1152]{1,0:T(8,128)(2,1)S(1)}, bf16[128,1152]{1,0:T(8,128)(2,1)S(1)}, u32[]{:S(2)}, u32[]{:S(2)}) collective-permute-start(bf16[128,1152]{1,0:T(8,128)(2,1)S(1)} %pad_maximum_fusion.2), channel_id=1, source_target_pairs={{0,2},{1,3},{2,0},{3,1},{4,6},{5,7},{6,4},{7,5},{8,10},{9,11},{10,... | collective-permute-start | bytes 884744 | tf_op jit(solution)/shard_map/ppermute | solution.py:308
  25.8 1.5 %collective-permute-start.10 = (bf16[128,1152]{1,0:T(8,128)(2,1)S(1)}, bf16[128,1152]{1,0:T(8,128)(2,1)S(1)}, u32[]{:S(2)}, u32[]{:S(2)}) collective-permute-start(bf16[128,1152]{1,0:T(8,128)(2,1)S(1)} %pad_maximum_fusion.2), channel_id=1, source_target_pairs={{0,4},{1,5},{2,6},{3,7},{4,0},{5,1},{6,2},{7,3},{8,12},{9,13},{10,... | collective-permute-start | bytes 884744 | tf_op jit(solution)/shard_map/ppermute | solution.py:308
  27.8 3.2 %collective-permute-start.8 = (bf16[256,384]{1,0:T(8,128)(2,1)S(1)}, bf16[256,384]{1,0:T(8,128)(2,1)S(1)}, u32[]{:S(2)}, u32[]{:S(2)}) collective-permute-start(bf16[256,384]{1,0:T(8,128)(2,1)S(1)} %pad_maximum_fusion.4), channel_id=1, source_target_pairs={{0,16},{1,17},{2,18},{3,19},{4,20},{5,21},{6,22},{7,23},{8,24},{9,... | collective-permute-start | bytes 589832 | tf_op jit(solution)/shard_map/ppermute | solution.py:308
  31.0 3.1 %collective-permute-done.9 = bf16[128,1152]{1,0:T(8,128)(2,1)S(1)} collective-permute-done((bf16[128,1152]{1,0:T(8,128)(2,1)S(1)}, bf16[128,1152]{1,0:T(8,128)(2,1)S(1)}, u32[]{:S(2)}, u32[]{:S(2)}) %collective-permute-start.9) | collective-permute-done | bytes 294944 | tf_op jit(solution)/shard_map/ppermute | solution.py:308
  34.1 4.0 %collective-permute-done.11 = bf16[128,1152]{1,0:T(8,128)(2,1)S(1)} collective-permute-done((bf16[128,1152]{1,0:T(8,128)(2,1)S(1)}, bf16[128,1152]{1,0:T(8,128)(2,1)S(1)}, u32[]{:S(2)}, u32[]{:S(2)}) %collective-permute-start.11) | collective-permute-done | bytes 294944 | tf_op jit(solution)/shard_map/ppermute | solution.py:308
  39.0 1.5 %collective-permute-start.17 = (bf16[512,384]{1,0:T(8,128)(2,1)S(1)}, bf16[512,384]{1,0:T(8,128)(2,1)S(1)}, u32[]{:S(2)}, u32[]{:S(2)}) collective-permute-start(bf16[512,384]{1,0:T(8,128)(2,1)S(1)} %pad_maximum_fusion.1), channel_id=1, source_target_pairs={{0,8},{1,9},{2,10},{3,11},{4,12},{5,13},{6,14},{7,15},{8,0},{9,1},... | collective-permute-start | bytes 1179656 | tf_op jit(solution)/shard_map/ppermute | solution.py:308
  40.5 1.5 %collective-permute-start.16 = (bf16[128,1152]{1,0:T(8,128)(2,1)S(1)}, bf16[128,1152]{1,0:T(8,128)(2,1)S(1)}, u32[]{:S(2)}, u32[]{:S(2)}) collective-permute-start(bf16[128,1152]{1,0:T(8,128)(2,1)S(1)} %pad_maximum_fusion.3.project_ref), channel_id=1, source_target_pairs={{0,6},{1,7},{2,4},{3,5},{4,2},{5,3},{6,0},{7,1},{8,14},{9,15},{10,... | collective-permute-start | bytes 884744 | tf_op jit(solution)/shard_map/ppermute | solution.py:308
  42.5 1.6 %grad.4.refs_0_ = bf16[128,1152]{1,0:T(8,128)(2,1)S(1)} custom-call(bf16[128,1152]{1,0:T(8,128)(2,1)S(1)} %pad_maximum_fusion.3.project_ref, bf16[512,1152]{1,0:T(8,128)(2,1)S(1)} %constant_dynamic-update-slice_fusion.refs_0_, bf16[512,1152]{1,0:T(8,128)(2,1)S(1)} %collective-permute-done.12.refs_1_), custom_call_target="tpu_custom_call" | custom-call | flops 603979776 | tf_op jit(solution)/shard_map/grad/pallas_call | solution.py:375
  44.1 9.9 %collective-permute-done.14.project_ref = bf16[128,1152]{1,0:T(8,128)(2,1)S(1)} collective-permute-done((bf16[128,1152]{1,0:T(8,128)(2,1)S(1)}, bf16[128,1152]{1,0:T(8,128)(2,1)S(1)}, u32[]{:S(2)}, u32[]{:S(2)}) %collective-permute-start.14) | collective-permute-done | bytes 294944 | tf_op jit(solution)/shard_map/ppermute | solution.py:308
  54.0 1.6 %grad.5.refs_2_ = bf16[128,1152]{1,0:T(8,128)(2,1)S(1)} custom-call(bf16[128,1152]{1,0:T(8,128)(2,1)S(1)} %collective-permute-done.14.project_ref, bf16[512,1152]{1,0:T(8,128)(2,1)S(1)} %constant_dynamic-update-slice_fusion.refs_0_, bf16[512,1152]{1,0:T(8,128)(2,1)S(1)} %collective-permute-done.12.refs_1_), custom_call_target="tpu_custom_call" | custom-call | flops 603979776 | tf_op jit(solution)/shard_map/grad/pallas_call | solution.py:375
  55.9 1.6 %grad.7.refs_0_ = bf16[128,1152]{1,0:T(8,128)(2,1)S(1)} custom-call(bf16[128,1152]{1,0:T(8,128)(2,1)S(1)} %collective-permute-done.19.project_ref, bf16[512,1152]{1,0:T(8,128)(2,1)S(1)} %constant_dynamic-update-slice_fusion.refs_0_, bf16[512,1152]{1,0:T(8,128)(2,1)S(1)} %collective-permute-done.12.refs_1_), custom_call_target="tpu_custom_call" | custom-call | flops 603979776 | tf_op jit(solution)/shard_map/grad/pallas_call | solution.py:375
  58.0 1.1 %grad_features.1 = bf16[128,384]{1,0:T(8,128)(2,1)} custom-call(s32[1]{0:T(128)} %bitcast.place_ref, bf16[384,1152]{1,0:T(8,128)(2,1)S(1)} %copy-done.1, f32[1,1152]{1,0:T(1,128)S(1)} %get-tuple-element.34.weight_sum_ref, bf16[128,1152]{1,0:T(8,128)(2,1)S(1)} %grad.4.refs_0_, bf16[128,1152]{1,0:T(8,128)(2,1)S(1)} %collective-permute-done.13.refs_1_, ...), custom_call_target="tpu_custom_call" | custom-call | flops 113246208 | tf_op jit(solution)/shard_map/grad_features/pallas_call | solution.py:408
  59.8 1.6 %grad.6.refs_0_ = bf16[128,1152]{1,0:T(8,128)(2,1)S(1)} custom-call(bf16[128,1152]{1,0:T(8,128)(2,1)S(1)} %collective-permute-done.16.project_ref, bf16[512,1152]{1,0:T(8,128)(2,1)S(1)} %constant_dynamic-update-slice_fusion.refs_0_, bf16[512,1152]{1,0:T(8,128)(2,1)S(1)} %collective-permute-done.12.refs_1_), custom_call_target="tpu_custom_call" | custom-call | flops 603979776 | tf_op jit(solution)/shard_map/grad/pallas_call | solution.py:375
  62.0 1.1 %collective-permute-done.18.refs_1_ = bf16[128,1152]{1,0:T(8,128)(2,1)S(1)} collective-permute-done((bf16[128,1152]{1,0:T(8,128)(2,1)S(1)}, bf16[128,1152]{1,0:T(8,128)(2,1)S(1)}, u32[]{:S(2)}, u32[]{:S(2)}) %collective-permute-start.18) | collective-permute-done | bytes 294944 | tf_op jit(solution)/shard_map/ppermute | solution.py:308
  63.1 1.5 %weight.5 = f32[384,1152]{1,0:T(8,128)} custom-call(s32[1]{0:T(128)} %bitcast.place_ref, bf16[1024,384]{1,0:T(8,128)(2,1)S(1)} %pad_maximum_fusion.normed_ref, bf16[128,1152]{1,0:T(8,128)(2,1)S(1)} %grad.6.refs_0_, bf16[128,1152]{1,0:T(8,128)(2,1)S(1)} %collective-permute-done.18.refs_1_, f32[384,1152]{1,0:T(8,128)S(1)} %weight.4.refs_2_), custom_call_target="tpu_custom_call" | custom-call | flops 226492416 | tf_op jit(solution)/shard_map/weight/pallas_call | solution.py:398
  (51 shorter events, 8.1 us)
Async XLA Ops:
  1.5 18.2 %copy-start.3 = (bf16[128,384]{1,0:T(8,128)(2,1)S(1)}, bf16[128,384]{1,0:T(8,128)(2,1)}, u32[]{:S(2)}) copy-start(bf16[128,384]{1,0:T(8,128)(2,1)} %features_ref.3) | copy-start | bytes 294916
  1.6 8.3 %collective-permute-start.3 = (bf16[32,1152]{1,0:T(8,128)(2,1)S(1)}, bf16[32,1152]{1,0:T(8,128)(2,1)S(1)}, u32[]{:S(2)}, u32[]{:S(2)}) collective-permute-start(bf16[32,1152]{1,0:T(8,128)(2,1)S(1)} %unit_texts.1), channel_id=1, source_target_pairs={{0,24},{1,25},{2,26},{3,27},{4,28},{5,29},{6,30},{7,31},{8,16},{9,... | collective-permute-start | bytes 221192 | tf_op jit(solution)/shard_map/ppermute | solution.py:308
  6.7 5.0 %collective-permute-start.2 = (bf16[32,1152]{1,0:T(8,128)(2,1)S(1)}, bf16[32,1152]{1,0:T(8,128)(2,1)S(1)}, u32[]{:S(2)}, u32[]{:S(2)}) collective-permute-start(bf16[32,1152]{1,0:T(8,128)(2,1)S(1)} %unit_texts.1), channel_id=1, source_target_pairs={{0,8},{1,9},{2,10},{3,11},{4,12},{5,13},{6,14},{7,15},{8,0},{9,1},... | collective-permute-start | bytes 221192 | tf_op jit(solution)/shard_map/ppermute | solution.py:308
  6.7 5.8 %collective-permute-start.1 = (bf16[32,1152]{1,0:T(8,128)(2,1)S(1)}, bf16[32,1152]{1,0:T(8,128)(2,1)S(1)}, u32[]{:S(2)}, u32[]{:S(2)}) collective-permute-start(bf16[32,1152]{1,0:T(8,128)(2,1)S(1)} %unit_texts.1), channel_id=1, source_target_pairs={{0,16},{1,17},{2,18},{3,19},{4,20},{5,21},{6,22},{7,23},{8,24},{9,... | collective-permute-start | bytes 221192 | tf_op jit(solution)/shard_map/ppermute | solution.py:308
  7.4 1.2 %copy-start = (bf16[384,1152]{1,0:T(8,128)(2,1)S(1)}, bf16[384,1152]{1,0:T(8,128)(2,1)}, u32[]{:S(2)}) copy-start(bf16[384,1152]{1,0:T(8,128)(2,1)} %weight_ref.3) | copy-start | bytes 2654212
  9.9 2.7 %collective-permute-start = (bf16[64,1280]{1,0:T(8,128)(2,1)S(1)}, bf16[64,1280]{1,0:T(8,128)(2,1)S(1)}, u32[]{:S(2)}, u32[]{:S(2)}) collective-permute-start(bf16[64,1280]{1,0:T(8,128)(2,1)S(1)} %get-tuple-element.26), channel_id=1, source_target_pairs={{0,1},{1,0},{2,3},{3,2},{4,5},{5,4},{6,7},{7,6},{8,9},{9,8},{10,11... | collective-permute-start | bytes 491528 | tf_op jit(solution)/shard_map/ppermute | solution.py:308
  12.7 4.5 %collective-permute-start.4 = (bf16[32,1280]{1,0:T(8,128)(2,1)S(1)}, bf16[32,1280]{1,0:T(8,128)(2,1)S(1)}, u32[]{:S(2)}, u32[]{:S(2)}) collective-permute-start(bf16[32,1280]{1,0:T(8,128)(2,1)S(1)} %get-tuple-element.31), channel_id=1, source_target_pairs={{0,2},{1,3},{2,0},{3,1},{4,6},{5,7},{6,4},{7,5},{8,10},{9,11},{10,... | collective-permute-start | bytes 245768 | tf_op jit(solution)/shard_map/ppermute | solution.py:308
  17.4 5.4 %collective-permute-start.5 = (bf16[32,1152]{1,0:T(8,128)(2,1)S(1)}, bf16[32,1152]{1,0:T(8,128)(2,1)S(1)}, u32[]{:S(2)}, u32[]{:S(2)}) collective-permute-start(bf16[32,1152]{1,0:T(8,128)(2,1)S(1)} %get-tuple-element.35), channel_id=1, source_target_pairs={{0,16},{1,17},{2,18},{3,19},{4,20},{5,21},{6,22},{7,23},{8,24},{9,... | collective-permute-start | bytes 221192 | tf_op jit(solution)/shard_map/ppermute | solution.py:308
  19.8 7.9 %collective-permute-start.7 = (bf16[128,384]{1,0:T(8,128)(2,1)S(1)}, bf16[128,384]{1,0:T(8,128)(2,1)S(1)}, u32[]{:S(2)}, u32[]{:S(2)}) collective-permute-start(bf16[128,384]{1,0:T(8,128)(2,1)S(1)} %centre.1), channel_id=1, source_target_pairs={{0,4},{1,5},{2,6},{3,7},{4,0},{5,1},{6,2},{7,3},{8,12},{9,13},{10,... | collective-permute-start | bytes 294920 | tf_op jit(solution)/shard_map/ppermute | solution.py:308
  22.8 8.2 %collective-permute-start.6 = (bf16[64,1152]{1,0:T(8,128)(2,1)S(1)}, bf16[64,1152]{1,0:T(8,128)(2,1)S(1)}, u32[]{:S(2)}, u32[]{:S(2)}) collective-permute-start(bf16[64,1152]{1,0:T(8,128)(2,1)S(1)} %pad_maximum_fusion.5), channel_id=1, source_target_pairs={{0,8},{1,9},{2,10},{3,11},{4,12},{5,13},{6,14},{7,15},{8,0},{9,1},... | collective-permute-start | bytes 442376 | tf_op jit(solution)/shard_map/ppermute | solution.py:308
  24.2 9.8 %collective-permute-start.9 = (bf16[128,1152]{1,0:T(8,128)(2,1)S(1)}, bf16[128,1152]{1,0:T(8,128)(2,1)S(1)}, u32[]{:S(2)}, u32[]{:S(2)}) collective-permute-start(bf16[128,1152]{1,0:T(8,128)(2,1)S(1)} %pad_maximum_fusion.2), channel_id=1, source_target_pairs={{0,2},{1,3},{2,0},{3,1},{4,6},{5,7},{6,4},{7,5},{8,10},{9,11},{10,... | collective-permute-start | bytes 884744 | tf_op jit(solution)/shard_map/ppermute | solution.py:308
  25.8 8.3 %collective-permute-start.10 = (bf16[128,1152]{1,0:T(8,128)(2,1)S(1)}, bf16[128,1152]{1,0:T(8,128)(2,1)S(1)}, u32[]{:S(2)}, u32[]{:S(2)}) collective-permute-start(bf16[128,1152]{1,0:T(8,128)(2,1)S(1)} %pad_maximum_fusion.2), channel_id=1, source_target_pairs={{0,4},{1,5},{2,6},{3,7},{4,0},{5,1},{6,2},{7,3},{8,12},{9,13},{10,... | collective-permute-start | bytes 884744 | tf_op jit(solution)/shard_map/ppermute | solution.py:308
  27.3 10.8 %collective-permute-start.11 = (bf16[128,1152]{1,0:T(8,128)(2,1)S(1)}, bf16[128,1152]{1,0:T(8,128)(2,1)S(1)}, u32[]{:S(2)}, u32[]{:S(2)}) collective-permute-start(bf16[128,1152]{1,0:T(8,128)(2,1)S(1)} %pad_maximum_fusion.2), channel_id=1, source_target_pairs={{0,6},{1,7},{2,4},{3,5},{4,2},{5,3},{6,0},{7,1},{8,14},{9,15},{10,... | collective-permute-start | bytes 884744 | tf_op jit(solution)/shard_map/ppermute | solution.py:308
  27.8 10.3 %collective-permute-start.8 = (bf16[256,384]{1,0:T(8,128)(2,1)S(1)}, bf16[256,384]{1,0:T(8,128)(2,1)S(1)}, u32[]{:S(2)}, u32[]{:S(2)}) collective-permute-start(bf16[256,384]{1,0:T(8,128)(2,1)S(1)} %pad_maximum_fusion.4), channel_id=1, source_target_pairs={{0,16},{1,17},{2,18},{3,19},{4,20},{5,21},{6,22},{7,23},{8,24},{9,... | collective-permute-start | bytes 589832 | tf_op jit(solution)/shard_map/ppermute | solution.py:308
  38.2 4.2 %collective-permute-start.12 = (bf16[512,1152]{1,0:T(8,128)(2,1)S(1)}, bf16[512,1152]{1,0:T(8,128)(2,1)S(1)}, u32[]{:S(2)}, u32[]{:S(2)}) collective-permute-start(bf16[512,1152]{1,0:T(8,128)(2,1)S(1)} %constant_dynamic-update-slice_fusion.refs_0_), channel_id=1, source_target_pairs={{0,1},{1,0},{2,3},{3,2},{4,5},{5,4},{6,7},{7,6},{8,9},{9,8},{10,11... | collective-permute-start | bytes 3538952 | tf_op jit(solution)/shard_map/ppermute | solution.py:308
  38.3 15.7 %collective-permute-start.14 = (bf16[128,1152]{1,0:T(8,128)(2,1)S(1)}, bf16[128,1152]{1,0:T(8,128)(2,1)S(1)}, u32[]{:S(2)}, u32[]{:S(2)}) collective-permute-start(bf16[128,1152]{1,0:T(8,128)(2,1)S(1)} %pad_maximum_fusion.3.project_ref), channel_id=1, source_target_pairs={{0,2},{1,3},{2,0},{3,1},{4,6},{5,7},{6,4},{7,5},{8,10},{9,11},{10,... | collective-permute-start | bytes 884744 | tf_op jit(solution)/shard_map/ppermute | solution.py:308
  39.0 16.7 %collective-permute-start.17 = (bf16[512,384]{1,0:T(8,128)(2,1)S(1)}, bf16[512,384]{1,0:T(8,128)(2,1)S(1)}, u32[]{:S(2)}, u32[]{:S(2)}) collective-permute-start(bf16[512,384]{1,0:T(8,128)(2,1)S(1)} %pad_maximum_fusion.1), channel_id=1, source_target_pairs={{0,8},{1,9},{2,10},{3,11},{4,12},{5,13},{6,14},{7,15},{8,0},{9,1},... | collective-permute-start | bytes 1179656 | tf_op jit(solution)/shard_map/ppermute | solution.py:308
  40.5 15.2 %collective-permute-start.16 = (bf16[128,1152]{1,0:T(8,128)(2,1)S(1)}, bf16[128,1152]{1,0:T(8,128)(2,1)S(1)}, u32[]{:S(2)}, u32[]{:S(2)}) collective-permute-start(bf16[128,1152]{1,0:T(8,128)(2,1)S(1)} %pad_maximum_fusion.3.project_ref), channel_id=1, source_target_pairs={{0,6},{1,7},{2,4},{3,5},{4,2},{5,3},{6,0},{7,1},{8,14},{9,15},{10,... | collective-permute-start | bytes 884744 | tf_op jit(solution)/shard_map/ppermute | solution.py:308
  42.1 13.8 %collective-permute-start.19 = (bf16[128,1152]{1,0:T(8,128)(2,1)S(1)}, bf16[128,1152]{1,0:T(8,128)(2,1)S(1)}, u32[]{:S(2)}, u32[]{:S(2)}) collective-permute-start(bf16[128,1152]{1,0:T(8,128)(2,1)S(1)} %pad_maximum_fusion.3.project_ref), channel_id=1, source_target_pairs={{0,4},{1,5},{2,6},{3,7},{4,0},{5,1},{6,2},{7,3},{8,12},{9,13},{10,... | collective-permute-start | bytes 884744 | tf_op jit(solution)/shard_map/ppermute | solution.py:308
  44.1 14.0 %collective-permute-start.13 = (bf16[128,1152]{1,0:T(8,128)(2,1)S(1)}, bf16[128,1152]{1,0:T(8,128)(2,1)S(1)}, u32[]{:S(2)}, u32[]{:S(2)}) collective-permute-start(bf16[128,1152]{1,0:T(8,128)(2,1)S(1)} %grad.4.refs_0_), channel_id=1, source_target_pairs={{0,1},{1,0},{2,3},{3,2},{4,5},{5,4},{6,7},{7,6},{8,9},{9,8},{10,11... | collective-permute-start | bytes 884744 | tf_op jit(solution)/shard_map/ppermute | solution.py:308
  55.7 2.4 %collective-permute-start.15 = (bf16[128,1152]{1,0:T(8,128)(2,1)S(1)}, bf16[128,1152]{1,0:T(8,128)(2,1)S(1)}, u32[]{:S(2)}, u32[]{:S(2)}) collective-permute-start(bf16[128,1152]{1,0:T(8,128)(2,1)S(1)} %grad.5.refs_2_), channel_id=1, source_target_pairs={{0,1},{1,0},{2,3},{3,2},{4,5},{5,4},{6,7},{7,6},{8,9},{9,8},{10,11... | collective-permute-start | bytes 884744 | tf_op jit(solution)/shard_map/ppermute | solution.py:308
  55.8 2.2 %copy-start.1 = (bf16[384,1152]{1,0:T(8,128)(2,1)S(1)}, bf16[384,1152]{1,0:T(8,128)(2,1)}, u32[]{:S(2)}) copy-start(bf16[384,1152]{1,0:T(8,128)(2,1)} %weight_ref.3) | copy-start | bytes 2654212
  57.5 4.1 %collective-permute-start.20 = (bf16[128,1152]{1,0:T(8,128)(2,1)S(1)}, bf16[128,1152]{1,0:T(8,128)(2,1)S(1)}, u32[]{:S(2)}, u32[]{:S(2)}) collective-permute-start(bf16[128,1152]{1,0:T(8,128)(2,1)S(1)} %grad.7.refs_0_), channel_id=1, source_target_pairs={{0,1},{1,0},{2,3},{3,2},{4,5},{5,4},{6,7},{7,6},{8,9},{9,8},{10,11... | collective-permute-start | bytes 884744 | tf_op jit(solution)/shard_map/ppermute | solution.py:308
  61.4 1.6 %collective-permute-start.18 = (bf16[128,1152]{1,0:T(8,128)(2,1)S(1)}, bf16[128,1152]{1,0:T(8,128)(2,1)S(1)}, u32[]{:S(2)}, u32[]{:S(2)}) collective-permute-start(bf16[128,1152]{1,0:T(8,128)(2,1)S(1)} %grad.6.refs_0_), channel_id=1, source_target_pairs={{0,1},{1,0},{2,3},{3,2},{4,5},{5,4},{6,7},{7,6},{8,9},{9,8},{10,11... | collective-permute-start | bytes 884744 | tf_op jit(solution)/shard_map/ppermute | solution.py:308
  (2 other events, 1.8 us)

commit v2 on v1

--- a/solution.py
+++ b/solution.py
@@ -341,7 +341,15 @@
         [unit_txt_b] + [swap(unit_txt_b, flip) for flip in order[1:]], axis=0
     )
     send, txt_line = lax.optimization_barrier((send, txt_line))
-    txt_plane = [txt_line] + [swap(txt_line, flip) for flip in plane[1:]]
+    middle = local_rows // 2
+
+    def diagonal(by_y, by_x):
+        return jnp.concatenate(
+            [swap(by_x[:middle], across), swap(by_y[middle:], column)], axis=0
+        )
+
+    txt_y, txt_x = swap(txt_line, across), swap(txt_line, column)
+    txt_plane = [txt_line, txt_y, txt_x, diagonal(txt_y, txt_x)]
 
     project, mean, weight_sum = kernel_call(
         functools.partial(rows_body, full_width, mp_count),
@@ -359,23 +367,23 @@
     line_rows = jnp.concatenate([line_rows, swap(line_rows, near)], axis=0)
     normed = jnp.concatenate([normed_b, swap(normed_b, column)], axis=0)
     normed_far = swap(normed, far)
-    line_rows, normed_far, *txt_plane = lax.optimization_barrier(
-        (line_rows, normed_far, *txt_plane)
+    line_rows, normed_far, txt_plane[1], txt_plane[2] = lax.optimization_barrier(
+        (line_rows, normed_far, txt_plane[1], txt_plane[2])
     )
     normed = jnp.concatenate([normed, normed_far], axis=0)
     normed_near = swap(normed, near)
     normed_order = sum([[o, o ^ column] for o in order], [])
     all_texts = [jnp.concatenate(txt_plane, axis=0)]
     all_texts.append(swap(all_texts[0], core))
-    plane_rows = [line_rows] + [swap(line_rows, flip) for flip in plane[1:3]]
-    last_rows = line_rows
-    plane_rows.append(swap(last_rows, plane[3]))
+    rows_y, rows_x = swap(line_rows, across), swap(line_rows, column)
+    diagonal_rows = [swap(rows_x[:middle], across), swap(rows_y[middle:], column)]
+    plane_rows = [line_rows, rows_y, rows_x]
 
     def gradient(index):
         return kernel_call(
             functools.partial(grad_body, index * local_rows),
             struct(line_rows.shape),
-            flops=4 * local_rows * count * rows * embed,
+            flops=0,
             name="grad",
         )(plane_rows[index], *all_texts)
 
@@ -384,7 +392,6 @@
     plane_rows[1], _ = lax.optimization_barrier((plane_rows[1], grads[0]))
     grads.append(gradient(1))
     others.append(swap(grads[1], core))
-    plane_rows[3], normed_near = lax.optimization_barrier((plane_rows[3], normed_near))
     normed = jnp.concatenate([normed, normed_near], axis=0)
 
     def add_product(indices, previous, final=False):
@@ -401,7 +408,7 @@
             scratch=scratch if final else (),
             in_specs=[smem] + [vmem] * (1 + len(arrays) + len(previous)),
             out_specs=pl.BlockSpec(memory_space=pl.ANY) if final else vmem,
-            flops=4 * width * embed * local_rows * len(indices),
+            flops=0 * 4 * width * embed * local_rows * len(indices),
             name="weight",
         )(place, normed, *arrays, *previous)
 
@@ -410,17 +417,20 @@
         struct(features.shape),
         scratch=[pltpu.VMEM((local_rows, embed), jnp.bfloat16)],
         in_specs=[smem] + [vmem] * (2 + mp_count),
-        flops=2 * local_rows * width * embed,
+        flops=0 * 2 * local_rows * width * embed,
         name="grad_features",
     )(place, proj_weight, weight_sum, grads[0], others[0], grads[1], others[1])
-    first = [0, 1]
+    first = [0]
     grad_weight = add_product(first, [])
     grads.append(gradient(2))
     others.append(swap(grads[2], core))
-    plane_rows[3], _, _ = lax.optimization_barrier((plane_rows[3], grad_weight, grad_features))
+    *diagonal_rows, _, _, _ = lax.optimization_barrier(
+        (*diagonal_rows, grads[2], grad_weight, grad_features)
+    )
+    plane_rows.append(jnp.concatenate(diagonal_rows, axis=0))
     grads.append(gradient(3))
     others.append(swap(grads[3], core))
-    grad_weight = add_product([2], [grad_weight])
+    grad_weight = add_product([1, 2], [grad_weight])
     grad_weight = add_product([3], [grad_weight], True)
     return grad_features, grad_weight
 

time: 64.8 us -> 61.3 us (0.946)
  waiting for transfers between devices: 24.9 us -> 22.7 us
  starting transfers between devices: 24.5 us -> 22.4 us
    ppermute x21 -> x23, waiting for transfers between devices: 24.9 us -> 22.7 us  [swap(): return lax.ppermute(value, axes, [(i, i ^ flip) for i in range(count)])]
    ppermute x21 -> x23, starting transfers between devices: 24.5 us -> 22.4 us  [swap(): return lax.ppermute(value, axes, [(i, i ^ flip) for i in range(count)])]
    unnamed x13 -> x14, local copies, waits for them, and re-layouts: 3.03 us -> 3.63 us
  transfers between devices with their start and end apart: 21 -> 23, of which waited for: 8 -> 10; matrix products, arithmetic and copies ran while one was open for 0% -> 1% of each run, Pallas kernels for 14% -> 15%
where the time goes in v2:
time: 61.3 us; the launch traced here: 61 us
  waiting for transfers between devices  22.7 us (37%)
  starting transfers between devices  22.4 us (37%)
  Pallas kernels  11.1 us (18%)
  local copies, waits for them, and re-layouts  3.7 us (6%)
  between operations  0.9 us (1%)
    ppermute x23, waiting for transfers between devices, swap(): return lax.ppermute(value, axes, [(i, i ^ flip) for i in range(count)])  22.7 us
    ppermute x23, starting transfers between devices, swap(): return lax.ppermute(value, axes, [(i, i ^ flip) for i in range(count)])  22.4 us
    pallas_call x4, Pallas kernels, gradient(): kernel_call(functools.partial(grad_body, index * local_rows), struct(line...  6.41 us
    unnamed x14, local copies, waits for them, and re-layouts  3.63 us
    pallas_call x3, Pallas kernels, add_product(): kernel_call(functools.partial(weight_body, rows, mp_count, normed_order,...  2.74 us
  transfers between devices with their start and end apart: 23, of which 10 were waited for; matrix products, arithmetic and copies ran while one was open for 1% of the time, Pallas kernels for 15%

profile of v2, /device:TPU:0, one launch (start us, length us, event | category | flops | bytes accessed | tf_op | source)
XLA Modules:
  0.0 61.0 jit_solution(2014669683552821050)
XLA Ops:
  0.6 0.9 %copy-done.4 = bf16[32,1152]{1,0:T(8,128)(2,1)S(1)} copy-done((bf16[32,1152]{1,0:T(8,128)(2,1)S(1)}, bf16[32,1152]{1,0:T(8,128)(2,1)}, u32[]{:S(2)}) %copy-start.4) | copy-done | bytes 73752
  1.6 5.1 %collective-permute-start.3 = (bf16[32,1152]{1,0:T(8,128)(2,1)S(1)}, bf16[32,1152]{1,0:T(8,128)(2,1)S(1)}, u32[]{:S(2)}, u32[]{:S(2)}) collective-permute-start(bf16[32,1152]{1,0:T(8,128)(2,1)S(1)} %unit_texts.1), channel_id=1, source_target_pairs={{0,24},{1,25},{2,26},{3,27},{4,28},{5,29},{6,30},{7,31},{8,16},{9,... | collective-permute-start | bytes 221192 | tf_op jit(solution)/shard_map/ppermute | solution.py:308
  7.4 1.2 %copy-done = bf16[384,1152]{1,0:T(8,128)(2,1)S(1)} copy-done((bf16[384,1152]{1,0:T(8,128)(2,1)S(1)}, bf16[384,1152]{1,0:T(8,128)(2,1)}, u32[]{:S(2)}) %copy-start) | copy-done | bytes 884760
  8.6 0.9 %copy-done.2 = bf16[128,384]{1,0:T(8,128)(2,1)S(1)} copy-done((bf16[128,384]{1,0:T(8,128)(2,1)S(1)}, bf16[128,384]{1,0:T(8,128)(2,1)}, u32[]{:S(2)}) %copy-start.2) | copy-done | bytes 98328
  9.9 1.8 %collective-permute-done.2 = bf16[32,1152]{1,0:T(8,128)(2,1)S(1)} collective-permute-done((bf16[32,1152]{1,0:T(8,128)(2,1)S(1)}, bf16[32,1152]{1,0:T(8,128)(2,1)S(1)}, u32[]{:S(2)}, u32[]{:S(2)}) %collective-permute-start.2) | collective-permute-done | bytes 73760 | tf_op jit(solution)/shard_map/ppermute | solution.py:308
  12.7 1.7 %collective-permute-start.4 = (bf16[32,1280]{1,0:T(8,128)(2,1)S(1)}, bf16[32,1280]{1,0:T(8,128)(2,1)S(1)}, u32[]{:S(2)}, u32[]{:S(2)}) collective-permute-start(bf16[32,1280]{1,0:T(8,128)(2,1)S(1)} %get-tuple-element.28), channel_id=1, source_target_pairs={{0,2},{1,3},{2,0},{3,1},{4,6},{5,7},{6,4},{7,5},{8,10},{9,11},{10,... | collective-permute-start | bytes 245768 | tf_op jit(solution)/shard_map/ppermute | solution.py:308
  14.4 2.8 %collective-permute-done.4.received_ref = bf16[32,1280]{1,0:T(8,128)(2,1)S(1)} collective-permute-done((bf16[32,1280]{1,0:T(8,128)(2,1)S(1)}, bf16[32,1280]{1,0:T(8,128)(2,1)S(1)}, u32[]{:S(2)}, u32[]{:S(2)}) %collective-permute-start.4) | collective-permute-done | bytes 81952 | tf_op jit(solution)/shard_map/ppermute | solution.py:308
  17.4 2.3 %collective-permute-start.5 = (bf16[32,1152]{1,0:T(8,128)(2,1)S(1)}, bf16[32,1152]{1,0:T(8,128)(2,1)S(1)}, u32[]{:S(2)}, u32[]{:S(2)}) collective-permute-start(bf16[32,1152]{1,0:T(8,128)(2,1)S(1)} %get-tuple-element.32), channel_id=1, source_target_pairs={{0,16},{1,17},{2,18},{3,19},{4,20},{5,21},{6,22},{7,23},{8,24},{9,... | collective-permute-start | bytes 221192 | tf_op jit(solution)/shard_map/ppermute | solution.py:308
  19.7 1.5 %collective-permute-start.9 = (bf16[128,1152]{1,0:T(8,128)(2,1)S(1)}, bf16[128,1152]{1,0:T(8,128)(2,1)S(1)}, u32[]{:S(2)}, u32[]{:S(2)}) collective-permute-start(bf16[128,1152]{1,0:T(8,128)(2,1)S(1)} %pad_maximum_fusion.2), channel_id=1, source_target_pairs={{0,2},{1,3},{2,0},{3,1},{4,6},{5,7},{6,4},{7,5},{8,10},{9,11},{10,... | collective-permute-start | bytes 884744 | tf_op jit(solution)/shard_map/ppermute | solution.py:308
  21.2 1.5 %collective-permute-start.10 = (bf16[128,1152]{1,0:T(8,128)(2,1)S(1)}, bf16[128,1152]{1,0:T(8,128)(2,1)S(1)}, u32[]{:S(2)}, u32[]{:S(2)}) collective-permute-start(bf16[128,1152]{1,0:T(8,128)(2,1)S(1)} %pad_maximum_fusion.2), channel_id=1, source_target_pairs={{0,4},{1,5},{2,6},{3,7},{4,0},{5,1},{6,2},{7,3},{8,12},{9,13},{10,... | collective-permute-start | bytes 884744 | tf_op jit(solution)/shard_map/ppermute | solution.py:308
  23.4 1.6 %collective-permute-start.6 = (bf16[64,1152]{1,0:T(8,128)(2,1)S(1)}, bf16[64,1152]{1,0:T(8,128)(2,1)S(1)}, u32[]{:S(2)}, u32[]{:S(2)}) collective-permute-start(bf16[64,1152]{1,0:T(8,128)(2,1)S(1)} %pad_maximum_fusion.6), channel_id=1, source_target_pairs={{0,8},{1,9},{2,10},{3,11},{4,12},{5,13},{6,14},{7,15},{8,0},{9,1},... | collective-permute-start | bytes 442376 | tf_op jit(solution)/shard_map/ppermute | solution.py:308
  25.0 4.7 %collective-permute-done.7 = bf16[128,384]{1,0:T(8,128)(2,1)S(1)} collective-permute-done((bf16[128,384]{1,0:T(8,128)(2,1)S(1)}, bf16[128,384]{1,0:T(8,128)(2,1)S(1)}, u32[]{:S(2)}, u32[]{:S(2)}) %collective-permute-start.7) | collective-permute-done | bytes 98336 | tf_op jit(solution)/shard_map/ppermute | solution.py:308
  30.8 1.7 %collective-permute-start.12 = (bf16[64,1152]{1,0:T(8,128)(2,1)S(1)}, bf16[64,1152]{1,0:T(8,128)(2,1)S(1)}, u32[]{:S(2)}, u32[]{:S(2)}) collective-permute-start(bf16[64,1152]{1,0:T(8,128)(2,1)S(1)} %slice.17), channel_id=1, source_target_pairs={{0,4},{1,5},{2,6},{3,7},{4,0},{5,1},{6,2},{7,3},{8,12},{9,13},{10,... | collective-permute-start | bytes 442376 | tf_op jit(solution)/shard_map/ppermute | solution.py:308
  32.5 5.9 %collective-permute-done.8 = bf16[256,384]{1,0:T(8,128)(2,1)S(1)} collective-permute-done((bf16[256,384]{1,0:T(8,128)(2,1)S(1)}, bf16[256,384]{1,0:T(8,128)(2,1)S(1)}, u32[]{:S(2)}, u32[]{:S(2)}) %collective-permute-start.8) | collective-permute-done | bytes 196640 | tf_op jit(solution)/shard_map/ppermute | solution.py:308
  39.5 1.5 %collective-permute-start.18 = (bf16[128,1152]{1,0:T(8,128)(2,1)S(1)}, bf16[128,1152]{1,0:T(8,128)(2,1)S(1)}, u32[]{:S(2)}, u32[]{:S(2)}) collective-permute-start(bf16[128,1152]{1,0:T(8,128)(2,1)S(1)} %pad_maximum_fusion.3.project_ref), channel_id=1, source_target_pairs={{0,4},{1,5},{2,6},{3,7},{4,0},{5,1},{6,2},{7,3},{8,12},{9,13},{10,... | collective-permute-start | bytes 884744 | tf_op jit(solution)/shard_map/ppermute | solution.py:308
  41.5 1.6 %grad.4.refs_0_ = bf16[128,1152]{1,0:T(8,128)(2,1)S(1)} custom-call(bf16[128,1152]{1,0:T(8,128)(2,1)S(1)} %pad_maximum_fusion.3.project_ref, bf16[512,1152]{1,0:T(8,128)(2,1)S(1)} %constant_dynamic-update-slice_fusion.refs_0_, bf16[512,1152]{1,0:T(8,128)(2,1)S(1)} %collective-permute-done.13.refs_1_), custom_call_target="tpu_custom_call" | custom-call | tf_op jit(solution)/shard_map/grad/pallas_call | solution.py:383
  43.3 4.8 %collective-permute-done.15.project_ref = bf16[128,1152]{1,0:T(8,128)(2,1)S(1)} collective-permute-done((bf16[128,1152]{1,0:T(8,128)(2,1)S(1)}, bf16[128,1152]{1,0:T(8,128)(2,1)S(1)}, u32[]{:S(2)}, u32[]{:S(2)}) %collective-permute-start.15) | collective-permute-done | bytes 294944 | tf_op jit(solution)/shard_map/ppermute | solution.py:308
  48.1 1.6 %grad.5.refs_2_.refs_0_ = bf16[128,1152]{1,0:T(8,128)(2,1)S(1)} custom-call(bf16[128,1152]{1,0:T(8,128)(2,1)S(1)} %collective-permute-done.15.project_ref, bf16[512,1152]{1,0:T(8,128)(2,1)S(1)} %constant_dynamic-update-slice_fusion.refs_0_, bf16[512,1152]{1,0:T(8,128)(2,1)S(1)} %collective-permute-done.13.refs_1_), custom_call_target="tpu_custom_call" | custom-call | tf_op jit(solution)/shard_map/grad/pallas_call | solution.py:383
  50.2 1.5 %collective-permute-start.20 = (bf16[64,1152]{1,0:T(8,128)(2,1)S(1)}, bf16[64,1152]{1,0:T(8,128)(2,1)S(1)}, u32[]{:S(2)}, u32[]{:S(2)}) collective-permute-start(bf16[64,1152]{1,0:T(8,128)(2,1)S(1)} %slice.19), channel_id=1, source_target_pairs={{0,4},{1,5},{2,6},{3,7},{4,0},{5,1},{6,2},{7,3},{8,12},{9,13},{10,... | collective-permute-start | bytes 442376 | tf_op jit(solution)/shard_map/ppermute | solution.py:308
  51.8 1.6 %grad.6.refs_2_ = bf16[128,1152]{1,0:T(8,128)(2,1)S(1)} custom-call(bf16[128,1152]{1,0:T(8,128)(2,1)S(1)} %collective-permute-done.18.project_ref, bf16[512,1152]{1,0:T(8,128)(2,1)S(1)} %constant_dynamic-update-slice_fusion.refs_0_, bf16[512,1152]{1,0:T(8,128)(2,1)S(1)} %collective-permute-done.13.refs_1_), custom_call_target="tpu_custom_call" | custom-call | tf_op jit(solution)/shard_map/grad/pallas_call | solution.py:383
  54.6 1.1 %grad_features.1 = bf16[128,384]{1,0:T(8,128)(2,1)} custom-call(s32[1]{0:T(128)} %bitcast.place_ref, bf16[384,1152]{1,0:T(8,128)(2,1)S(1)} %copy-done.1, f32[1,1152]{1,0:T(1,128)S(1)} %get-tuple-element.31.weight_sum_ref, bf16[128,1152]{1,0:T(8,128)(2,1)S(1)} %grad.4.refs_0_, bf16[128,1152]{1,0:T(8,128)(2,1)S(1)} %collective-permute-done.14.refs_1_, ...), custom_call_target="tpu_custom_call" | custom-call | tf_op jit(solution)/shard_map/grad_features/pallas_call | solution.py:415
  56.2 1.6 %grad.7.refs_0_ = bf16[128,1152]{1,0:T(8,128)(2,1)S(1)} custom-call(bf16[128,1152]{1,0:T(8,128)(2,1)S(1)} %pad_maximum_fusion.4.project_ref, bf16[512,1152]{1,0:T(8,128)(2,1)S(1)} %constant_dynamic-update-slice_fusion.refs_0_, bf16[512,1152]{1,0:T(8,128)(2,1)S(1)} %collective-permute-done.13.refs_1_), custom_call_target="tpu_custom_call" | custom-call | tf_op jit(solution)/shard_map/grad/pallas_call | solution.py:383
  58.7 0.8 %collective-permute-done.21.refs_1_ = bf16[128,1152]{1,0:T(8,128)(2,1)S(1)} collective-permute-done((bf16[128,1152]{1,0:T(8,128)(2,1)S(1)}, bf16[128,1152]{1,0:T(8,128)(2,1)S(1)}, u32[]{:S(2)}, u32[]{:S(2)}) %collective-permute-start.21) | collective-permute-done | bytes 294944 | tf_op jit(solution)/shard_map/ppermute | solution.py:308
  59.5 1.5 %weight.5 = f32[384,1152]{1,0:T(8,128)} custom-call(s32[1]{0:T(128)} %bitcast.place_ref, bf16[1024,384]{1,0:T(8,128)(2,1)S(1)} %pad_maximum_fusion.normed_ref, bf16[128,1152]{1,0:T(8,128)(2,1)S(1)} %grad.7.refs_0_, bf16[128,1152]{1,0:T(8,128)(2,1)S(1)} %collective-permute-done.21.refs_1_, f32[384,1152]{1,0:T(8,128)S(1)} %weight.4.refs_2_), custom_call_target="tpu_custom_call" | custom-call | tf_op jit(solution)/shard_map/weight/pallas_call | solution.py:405
  (61 shorter events, 8.9 us)
Async XLA Ops:
  1.5 21.2 %copy-start.3 = (bf16[128,384]{1,0:T(8,128)(2,1)S(1)}, bf16[128,384]{1,0:T(8,128)(2,1)}, u32[]{:S(2)}) copy-start(bf16[128,384]{1,0:T(8,128)(2,1)} %features_ref.3) | copy-start | bytes 294916
  1.6 8.3 %collective-permute-start.3 = (bf16[32,1152]{1,0:T(8,128)(2,1)S(1)}, bf16[32,1152]{1,0:T(8,128)(2,1)S(1)}, u32[]{:S(2)}, u32[]{:S(2)}) collective-permute-start(bf16[32,1152]{1,0:T(8,128)(2,1)S(1)} %unit_texts.1), channel_id=1, source_target_pairs={{0,24},{1,25},{2,26},{3,27},{4,28},{5,29},{6,30},{7,31},{8,16},{9,... | collective-permute-start | bytes 221192 | tf_op jit(solution)/shard_map/ppermute | solution.py:308
  6.7 5.0 %collective-permute-start.2 = (bf16[32,1152]{1,0:T(8,128)(2,1)S(1)}, bf16[32,1152]{1,0:T(8,128)(2,1)S(1)}, u32[]{:S(2)}, u32[]{:S(2)}) collective-permute-start(bf16[32,1152]{1,0:T(8,128)(2,1)S(1)} %unit_texts.1), channel_id=1, source_target_pairs={{0,8},{1,9},{2,10},{3,11},{4,12},{5,13},{6,14},{7,15},{8,0},{9,1},... | collective-permute-start | bytes 221192 | tf_op jit(solution)/shard_map/ppermute | solution.py:308
  6.7 5.8 %collective-permute-start.1 = (bf16[32,1152]{1,0:T(8,128)(2,1)S(1)}, bf16[32,1152]{1,0:T(8,128)(2,1)S(1)}, u32[]{:S(2)}, u32[]{:S(2)}) collective-permute-start(bf16[32,1152]{1,0:T(8,128)(2,1)S(1)} %unit_texts.1), channel_id=1, source_target_pairs={{0,16},{1,17},{2,18},{3,19},{4,20},{5,21},{6,22},{7,23},{8,24},{9,... | collective-permute-start | bytes 221192 | tf_op jit(solution)/shard_map/ppermute | solution.py:308
  9.9 2.7 %collective-permute-start = (bf16[64,1280]{1,0:T(8,128)(2,1)S(1)}, bf16[64,1280]{1,0:T(8,128)(2,1)S(1)}, u32[]{:S(2)}, u32[]{:S(2)}) collective-permute-start(bf16[64,1280]{1,0:T(8,128)(2,1)S(1)} %get-tuple-element.23), channel_id=1, source_target_pairs={{0,1},{1,0},{2,3},{3,2},{4,5},{5,4},{6,7},{7,6},{8,9},{9,8},{10,11... | collective-permute-start | bytes 491528 | tf_op jit(solution)/shard_map/ppermute | solution.py:308
  12.7 4.5 %collective-permute-start.4 = (bf16[32,1280]{1,0:T(8,128)(2,1)S(1)}, bf16[32,1280]{1,0:T(8,128)(2,1)S(1)}, u32[]{:S(2)}, u32[]{:S(2)}) collective-permute-start(bf16[32,1280]{1,0:T(8,128)(2,1)S(1)} %get-tuple-element.28), channel_id=1, source_target_pairs={{0,2},{1,3},{2,0},{3,1},{4,6},{5,7},{6,4},{7,5},{8,10},{9,11},{10,... | collective-permute-start | bytes 245768 | tf_op jit(solution)/shard_map/ppermute | solution.py:308
  17.4 6.0 %collective-permute-start.5 = (bf16[32,1152]{1,0:T(8,128)(2,1)S(1)}, bf16[32,1152]{1,0:T(8,128)(2,1)S(1)}, u32[]{:S(2)}, u32[]{:S(2)}) collective-permute-start(bf16[32,1152]{1,0:T(8,128)(2,1)S(1)} %get-tuple-element.32), channel_id=1, source_target_pairs={{0,16},{1,17},{2,18},{3,19},{4,20},{5,21},{6,22},{7,23},{8,24},{9,... | collective-permute-start | bytes 221192 | tf_op jit(solution)/shard_map/ppermute | solution.py:308
  19.7 11.1 %collective-permute-start.9 = (bf16[128,1152]{1,0:T(8,128)(2,1)S(1)}, bf16[128,1152]{1,0:T(8,128)(2,1)S(1)}, u32[]{:S(2)}, u32[]{:S(2)}) collective-permute-start(bf16[128,1152]{1,0:T(8,128)(2,1)S(1)} %pad_maximum_fusion.2), channel_id=1, source_target_pairs={{0,2},{1,3},{2,0},{3,1},{4,6},{5,7},{6,4},{7,5},{8,10},{9,11},{10,... | collective-permute-start | bytes 884744 | tf_op jit(solution)/shard_map/ppermute | solution.py:308
  21.2 9.1 %collective-permute-start.10 = (bf16[128,1152]{1,0:T(8,128)(2,1)S(1)}, bf16[128,1152]{1,0:T(8,128)(2,1)S(1)}, u32[]{:S(2)}, u32[]{:S(2)}) collective-permute-start(bf16[128,1152]{1,0:T(8,128)(2,1)S(1)} %pad_maximum_fusion.2), channel_id=1, source_target_pairs={{0,4},{1,5},{2,6},{3,7},{4,0},{5,1},{6,2},{7,3},{8,12},{9,13},{10,... | collective-permute-start | bytes 884744 | tf_op jit(solution)/shard_map/ppermute | solution.py:308
  22.8 6.9 %collective-permute-start.7 = (bf16[128,384]{1,0:T(8,128)(2,1)S(1)}, bf16[128,384]{1,0:T(8,128)(2,1)S(1)}, u32[]{:S(2)}, u32[]{:S(2)}) collective-permute-start(bf16[128,384]{1,0:T(8,128)(2,1)S(1)} %centre.1), channel_id=1, source_target_pairs={{0,4},{1,5},{2,6},{3,7},{4,0},{5,1},{6,2},{7,3},{8,12},{9,13},{10,... | collective-permute-start | bytes 294920 | tf_op jit(solution)/shard_map/ppermute | solution.py:308
  23.4 9.0 %collective-permute-start.6 = (bf16[64,1152]{1,0:T(8,128)(2,1)S(1)}, bf16[64,1152]{1,0:T(8,128)(2,1)S(1)}, u32[]{:S(2)}, u32[]{:S(2)}) collective-permute-start(bf16[64,1152]{1,0:T(8,128)(2,1)S(1)} %pad_maximum_fusion.6), channel_id=1, source_target_pairs={{0,8},{1,9},{2,10},{3,11},{4,12},{5,13},{6,14},{7,15},{8,0},{9,1},... | collective-permute-start | bytes 442376 | tf_op jit(solution)/shard_map/ppermute | solution.py:308
  29.7 8.7 %collective-permute-start.8 = (bf16[256,384]{1,0:T(8,128)(2,1)S(1)}, bf16[256,384]{1,0:T(8,128)(2,1)S(1)}, u32[]{:S(2)}, u32[]{:S(2)}) collective-permute-start(bf16[256,384]{1,0:T(8,128)(2,1)S(1)} %pad_maximum_fusion.5), channel_id=1, source_target_pairs={{0,16},{1,17},{2,18},{3,19},{4,20},{5,21},{6,22},{7,23},{8,24},{9,... | collective-permute-start | bytes 589832 | tf_op jit(solution)/shard_map/ppermute | solution.py:308
  30.3 8.2 %collective-permute-start.11 = (bf16[64,1152]{1,0:T(8,128)(2,1)S(1)}, bf16[64,1152]{1,0:T(8,128)(2,1)S(1)}, u32[]{:S(2)}, u32[]{:S(2)}) collective-permute-start(bf16[64,1152]{1,0:T(8,128)(2,1)S(1)} %slice.16), channel_id=1, source_target_pairs={{0,2},{1,3},{2,0},{3,1},{4,6},{5,7},{6,4},{7,5},{8,10},{9,11},{10,... | collective-permute-start | bytes 442376 | tf_op jit(solution)/shard_map/ppermute | solution.py:308
  30.8 7.8 %collective-permute-start.12 = (bf16[64,1152]{1,0:T(8,128)(2,1)S(1)}, bf16[64,1152]{1,0:T(8,128)(2,1)S(1)}, u32[]{:S(2)}, u32[]{:S(2)}) collective-permute-start(bf16[64,1152]{1,0:T(8,128)(2,1)S(1)} %slice.17), channel_id=1, source_target_pairs={{0,4},{1,5},{2,6},{3,7},{4,0},{5,1},{6,2},{7,3},{8,12},{9,13},{10,... | collective-permute-start | bytes 442376 | tf_op jit(solution)/shard_map/ppermute | solution.py:308
  38.6 2.9 %collective-permute-start.13 = (bf16[512,1152]{1,0:T(8,128)(2,1)S(1)}, bf16[512,1152]{1,0:T(8,128)(2,1)S(1)}, u32[]{:S(2)}, u32[]{:S(2)}) collective-permute-start(bf16[512,1152]{1,0:T(8,128)(2,1)S(1)} %constant_dynamic-update-slice_fusion.refs_0_), channel_id=1, source_target_pairs={{0,1},{1,0},{2,3},{3,2},{4,5},{5,4},{6,7},{7,6},{8,9},{9,8},{10,11... | collective-permute-start | bytes 3538952 | tf_op jit(solution)/shard_map/ppermute | solution.py:308
  38.7 9.4 %collective-permute-start.15 = (bf16[128,1152]{1,0:T(8,128)(2,1)S(1)}, bf16[128,1152]{1,0:T(8,128)(2,1)S(1)}, u32[]{:S(2)}, u32[]{:S(2)}) collective-permute-start(bf16[128,1152]{1,0:T(8,128)(2,1)S(1)} %pad_maximum_fusion.3.project_ref), channel_id=1, source_target_pairs={{0,2},{1,3},{2,0},{3,1},{4,6},{5,7},{6,4},{7,5},{8,10},{9,11},{10,... | collective-permute-start | bytes 884744 | tf_op jit(solution)/shard_map/ppermute | solution.py:308
  39.0 12.7 %collective-permute-start.17 = (bf16[512,384]{1,0:T(8,128)(2,1)S(1)}, bf16[512,384]{1,0:T(8,128)(2,1)S(1)}, u32[]{:S(2)}, u32[]{:S(2)}) collective-permute-start(bf16[512,384]{1,0:T(8,128)(2,1)S(1)} %pad_maximum_fusion.1), channel_id=1, source_target_pairs={{0,8},{1,9},{2,10},{3,11},{4,12},{5,13},{6,14},{7,15},{8,0},{9,1},... | collective-permute-start | bytes 1179656 | tf_op jit(solution)/shard_map/ppermute | solution.py:308
  39.5 10.3 %collective-permute-start.18 = (bf16[128,1152]{1,0:T(8,128)(2,1)S(1)}, bf16[128,1152]{1,0:T(8,128)(2,1)S(1)}, u32[]{:S(2)}, u32[]{:S(2)}) collective-permute-start(bf16[128,1152]{1,0:T(8,128)(2,1)S(1)} %pad_maximum_fusion.3.project_ref), channel_id=1, source_target_pairs={{0,4},{1,5},{2,6},{3,7},{4,0},{5,1},{6,2},{7,3},{8,12},{9,13},{10,... | collective-permute-start | bytes 884744 | tf_op jit(solution)/shard_map/ppermute | solution.py:308
  43.1 10.4 %collective-permute-start.14 = (bf16[128,1152]{1,0:T(8,128)(2,1)S(1)}, bf16[128,1152]{1,0:T(8,128)(2,1)S(1)}, u32[]{:S(2)}, u32[]{:S(2)}) collective-permute-start(bf16[128,1152]{1,0:T(8,128)(2,1)S(1)} %grad.4.refs_0_), channel_id=1, source_target_pairs={{0,1},{1,0},{2,3},{3,2},{4,5},{5,4},{6,7},{7,6},{8,9},{9,8},{10,11... | collective-permute-start | bytes 884744 | tf_op jit(solution)/shard_map/ppermute | solution.py:308
  49.7 4.3 %collective-permute-start.16 = (bf16[128,1152]{1,0:T(8,128)(2,1)S(1)}, bf16[128,1152]{1,0:T(8,128)(2,1)S(1)}, u32[]{:S(2)}, u32[]{:S(2)}) collective-permute-start(bf16[128,1152]{1,0:T(8,128)(2,1)S(1)} %grad.5.refs_2_.refs_0_), channel_id=1, source_target_pairs={{0,1},{1,0},{2,3},{3,2},{4,5},{5,4},{6,7},{7,6},{8,9},{9,8},{10,11... | collective-permute-start | bytes 884744 | tf_op jit(solution)/shard_map/ppermute | solution.py:308
  49.8 6.3 %collective-permute-start.19 = (bf16[64,1152]{1,0:T(8,128)(2,1)S(1)}, bf16[64,1152]{1,0:T(8,128)(2,1)S(1)}, u32[]{:S(2)}, u32[]{:S(2)}) collective-permute-start(bf16[64,1152]{1,0:T(8,128)(2,1)S(1)} %slice.18), channel_id=1, source_target_pairs={{0,2},{1,3},{2,0},{3,1},{4,6},{5,7},{6,4},{7,5},{8,10},{9,11},{10,... | collective-permute-start | bytes 442376 | tf_op jit(solution)/shard_map/ppermute | solution.py:308
  50.2 6.1 %collective-permute-start.20 = (bf16[64,1152]{1,0:T(8,128)(2,1)S(1)}, bf16[64,1152]{1,0:T(8,128)(2,1)S(1)}, u32[]{:S(2)}, u32[]{:S(2)}) collective-permute-start(bf16[64,1152]{1,0:T(8,128)(2,1)S(1)} %slice.19), channel_id=1, source_target_pairs={{0,4},{1,5},{2,6},{3,7},{4,0},{5,1},{6,2},{7,3},{8,12},{9,13},{10,... | collective-permute-start | bytes 442376 | tf_op jit(solution)/shard_map/ppermute | solution.py:308
  53.4 4.5 %collective-permute-start.22 = (bf16[128,1152]{1,0:T(8,128)(2,1)S(1)}, bf16[128,1152]{1,0:T(8,128)(2,1)S(1)}, u32[]{:S(2)}, u32[]{:S(2)}) collective-permute-start(bf16[128,1152]{1,0:T(8,128)(2,1)S(1)} %grad.6.refs_2_), channel_id=1, source_target_pairs={{0,1},{1,0},{2,3},{3,2},{4,5},{5,4},{6,7},{7,6},{8,9},{9,8},{10,11... | collective-permute-start | bytes 884744 | tf_op jit(solution)/shard_map/ppermute | solution.py:308
  57.9 1.6 %collective-permute-start.21 = (bf16[128,1152]{1,0:T(8,128)(2,1)S(1)}, bf16[128,1152]{1,0:T(8,128)(2,1)S(1)}, u32[]{:S(2)}, u32[]{:S(2)}) collective-permute-start(bf16[128,1152]{1,0:T(8,128)(2,1)S(1)} %grad.7.refs_0_), channel_id=1, source_target_pairs={{0,1},{1,0},{2,3},{3,2},{4,5},{5,4},{6,7},{7,6},{8,9},{9,8},{10,11... | collective-permute-start | bytes 884744 | tf_op jit(solution)/shard_map/ppermute | solution.py:308
  (4 other events, 4.1 us)
